TPU v7x, 512 devices: a whole 4x4x16 slice. The times are simulated.
512 devices in a mesh: slab: 32 (over y, z_lo), row: 16 (over z_hi, x, core).
Axes of the slice: x: 4, y: 4, z: 16 (z_hi: 2, z_lo: 8; z = z_hi * 8 + z_lo), core: 2. Of those that a mesh axis runs over, the one named last changes fastest.
Arguments:
- queries: bfloat16 [32768, 32, 128], P('slab', 'row'), may hold values from -72 to 72, as said below
- keys: bfloat16 [32768, 32, 128], P('slab', 'row'), may hold values from -4 to 4
- values: bfloat16 [32768, 32, 128], P('slab', 'row'), may hold values from -6 to 6
- out_grad: bfloat16 [32768, 32, 128], P(('slab', 'row')), may hold values from -6 to 6
- col_start: int32 [256], replicated, may hold values from 0 to 2, as said below
- valid_tiles: int32 [32], replicated, may hold values from 4 to 8, as said below
Outputs:
- query_grad: bfloat16 [32768, 32, 128], P(('slab', 'row'))
- key_grad: bfloat16 [32768, 32, 128], P(('slab', 'row'))
- value_grad: bfloat16 [32768, 32, 128], P(('slab', 'row'))
Inputs may be any that keep to these rules, and one draw needn't show every extreme that they name: `queries`: of order one in most rows. For query tile a with tile column w = (a % 8) % 4, col_start[a] is w - 1 or w, kept within 0 to 2. The tiles of a slab with index below valid_tiles hold real keys, the others padding; the values 4 and 8 occur in every draw.
All inputs are finite; a program needn't handle non-finite values.
Results may differ from a plain program's by a relative error of at most 0.0095.
Values may be sent and summed in bfloat16 or wider, within the bound.
A program may use at most 128 MiB of HBM per device.

v0:
```python
import jax
import jax.numpy as jnp
from jax import lax
from jax.sharding import PartitionSpec as P

TILE = 128
GH = 2
GW = 4
WIN_COLS = 2
TPS = 8


def padded(block, sides, width):
    for axis, dim in sides:
        count = lax.axis_size(axis)
        forward = [(i, i + 1) for i in range(count - 1)]
        backward = [(target, source) for source, target in forward]
        low = lax.ppermute(
            lax.slice_in_dim(block, block.shape[dim] - width, None, axis=dim), axis, forward
        )
        high = lax.ppermute(lax.slice_in_dim(block, 0, width, axis=dim), axis, backward)
        block = jnp.concatenate([low, block, high], axis=dim)
    return block


def from_behind(value, axis, steps):
    count = lax.axis_size(axis)
    leading, last = (max(0, -steps), min(count, count - steps))
    return lax.ppermute(value, axis, [(source, source + steps) for source in range(leading, last)])


def tile_slots(offset_count):
    per_row = GH * WIN_COLS
    slot_ids = jnp.arange(offset_count * per_row, dtype=jnp.int32)
    slab_step = slot_ids // per_row
    inner_slot = slot_ids % per_row
    tile_base = slab_step * TPS + inner_slot // WIN_COLS * GW + inner_slot % WIN_COLS
    return (tile_base, slab_step)


def slab_counts(key_slab, valid_tiles):
    slab_ids = jnp.arange(valid_tiles.shape[0], dtype=jnp.int32)
    return jnp.sum(
        jnp.where(slab_ids[None, :] == key_slab[:, None], valid_tiles[None, :], 0), axis=1
    )


def pick_keys(tile_array, key_tiles, key_valid):
    tile_count, slot_count = key_tiles.shape
    tile_len = tile_array.shape[2]
    key_sel = tile_array[0][key_tiles]
    value_sel = tile_array[1][key_tiles]
    wide_shape = (tile_count, slot_count * tile_len) + key_sel.shape[3:]
    valid_wide = jnp.repeat(key_valid, tile_len, axis=1)[:, None, None, :]
    return (key_sel.reshape(wide_shape), value_sel.reshape(wide_shape), valid_wide)


def forward_block(query_block, grad_rows, key_sel, value_sel, valid_wide, inv_root):
    scores = (
        jnp.einsum("nqhd,nkhd->nhqk", query_block, key_sel, preferred_element_type=jnp.float32)
        * inv_root
    )
    scores = jnp.where(valid_wide, scores, -jnp.inf)
    row_max = jnp.max(scores, axis=-1, keepdims=True)
    expo_vals = jnp.exp(scores - row_max)
    row_total = jnp.sum(expo_vals, axis=-1, keepdims=True)
    attend = expo_vals / row_total
    attend_b = attend.astype(jnp.bfloat16)
    output = jnp.einsum("nhqk,nkhd->nqhd", attend_b, value_sel, preferred_element_type=jnp.float32)
    row_delta = jnp.einsum("nqhd,nqhd->nhq", grad_rows.astype(jnp.float32), output)
    log_total = row_max[..., 0] + jnp.log(row_total[..., 0])
    return (attend, attend_b, row_delta, log_total)


def backward_block(
    query_block, grad_rows, key_sel, value_sel, attend, attend_b, row_delta, inv_root
):
    grad_attend = jnp.einsum(
        "nqhd,nkhd->nhqk", grad_rows, value_sel, preferred_element_type=jnp.float32
    )
    grad_scores = (attend * (grad_attend - row_delta[..., None])).astype(jnp.bfloat16)
    query_grad = None
    query_grad = (
        jnp.einsum("nhqk,nkhd->nqhd", grad_scores, key_sel, preferred_element_type=jnp.float32)
        * inv_root
    )
    key_grad = (
        jnp.einsum("nhqk,nqhd->nkhd", grad_scores, query_block, preferred_element_type=jnp.float32)
        * inv_root
    )
    value_grad = jnp.einsum(
        "nhqk,nqhd->nkhd", attend_b, grad_rows, preferred_element_type=jnp.float32
    )
    return (query_grad, key_grad, value_grad)


def on_device(queries, keys, values, out_grad, col_start, valid_tiles):
    tok_slab, heads_here, head_dim = queries.shape
    inv_root = head_dim ** (-0.5)
    slab_total = valid_tiles.shape[0]
    slab_pos = lax.axis_index("slab")
    grad_local = lax.all_to_all(out_grad, "row", split_axis=1, concat_axis=0, tiled=True)
    key_pair = jnp.stack([keys, values])
    wide_pair = padded(key_pair, (("slab", 1),), tok_slab)
    tile_shape = (TILE, heads_here, head_dim)
    wide_tiles = wide_pair.reshape((2, 3 * TPS) + tile_shape)
    col_first = lax.dynamic_slice_in_dim(col_start, slab_pos * TPS, TPS, 0)
    tile_base, slab_step = tile_slots(3)
    key_tiles = tile_base[None, :] + col_first[:, None]
    key_slab = slab_pos - 1 + slab_step
    counts = slab_counts(key_slab, valid_tiles)
    key_valid = (
        (key_slab[None, :] >= 0)
        & (key_slab[None, :] < slab_total)
        & (key_tiles - slab_step[None, :] * TPS < counts[None, :])
    )
    row_inputs = (
        queries.reshape((GH, GW) + tile_shape),
        grad_local.reshape((GH, GW) + tile_shape),
        key_tiles.reshape(GH, GW, -1),
        key_valid.reshape(GH, GW, -1),
    )

    def row_step(partial_value, inputs):
        query_block, grad_rows, block_tiles, block_valid = inputs
        key_sel, value_sel, valid_wide = pick_keys(wide_tiles, block_tiles, block_valid)
        attend, attend_b, row_delta, log_total = forward_block(
            query_block, grad_rows, key_sel, value_sel, valid_wide, inv_root
        )
        query_grad, key_grad, value_grad = backward_block(
            query_block, grad_rows, key_sel, value_sel, attend, attend_b, row_delta, inv_root
        )
        tile_count, slot_count = block_tiles.shape
        both_grads = jnp.stack([key_grad, value_grad]).reshape(
            (2, tile_count, slot_count) + tile_shape
        )
        return (partial_value.at[:, block_tiles].add(both_grads), query_grad)

    start_sums = jnp.zeros((2, 3 * TPS) + tile_shape, jnp.float32)
    partial_value, query_rows = lax.scan(row_step, start_sums, row_inputs)
    flat_grads = partial_value.reshape(2, 3 * tok_slab, heads_here, head_dim)
    lower_part = from_behind(flat_grads[:, :tok_slab], "slab", -1)
    upper_part = from_behind(flat_grads[:, 2 * tok_slab :], "slab", 1)
    grad_sums = flat_grads[:, tok_slab : 2 * tok_slab] + lower_part + upper_part
    query_grad = query_rows.reshape(tok_slab, heads_here, head_dim).astype(jnp.bfloat16)
    key_grad = grad_sums[0].astype(jnp.bfloat16)
    value_grad = grad_sums[1].astype(jnp.bfloat16)
    return (
        lax.all_to_all(query_grad, "row", split_axis=0, concat_axis=1, tiled=True),
        lax.all_to_all(key_grad, "row", split_axis=0, concat_axis=1, tiled=True),
        lax.all_to_all(value_grad, "row", split_axis=0, concat_axis=1, tiled=True),
    )


def solution(mesh):
    placed = (
        P("slab", "row", None),
        P("slab", "row", None),
        P("slab", "row", None),
        P(("slab", "row"), None, None),
        P(),
        P(),
    )
    return jax.shard_map(
        on_device,
        mesh=mesh,
        in_specs=placed,
        out_specs=(
            P(("slab", "row"), None, None),
            P(("slab", "row"), None, None),
            P(("slab", "row"), None, None),
        ),
        check_vma=False,
    )
```

profile of v0, /device:TPU:8, one launch (start us, length us, event | category | flops | bytes accessed | tf_op | source)
XLA Modules:
  0.0 591.7 jit_solution(6449510817472611369)
XLA Ops:
  3.5 13.0 %collective-permute-start.1 = (bf16[2,1024,2,128]{3,2,1,0:T(2,128)(2,1)S(1)}, bf16[2,1024,2,128]{3,2,1,0:T(2,128)(2,1)}, u32[]{:S(2)}, u32[]{:S(2)}) collective-permute-start(bf16[2,1024,2,128]{3,2,1,0:T(2,128)(2,1)S(1)} %pad_maximum_fusion.1), channel_id=1, source_target_pairs={{16,0},{32,16},{48,32},{64,48},{80,64},{96,80},{112,96},{128,112},... | collective-permute-start | bytes 3145736 | tf_op jit(solution)/shard_map/ppermute | solution.py:21
  20.6 10.2 %all-to-all-start = ((bf16[64,32,128]{2,0,1:T(8,128)(2,1)}), bf16[64,32,128]{2,0,1:T(8,128)(2,1)S(1)}, u32[]{:S(2)}, u32[]{:S(2)}) async-start(bf16[64,32,128]{2,0,1:T(8,128)(2,1)} %copy.87), calls=%async_computation | async-start | bytes 1048576 | tf_op jit(solution)/shard_map/all_to_all | solution.py:102
  31.3 8.8 %collective-permute-done.1 = bf16[2,1024,2,128]{3,2,1,0:T(2,128)(2,1)} collective-permute-done((bf16[2,1024,2,128]{3,2,1,0:T(2,128)(2,1)S(1)}, bf16[2,1024,2,128]{3,2,1,0:T(2,128)(2,1)}, u32[]{:S(2)}, u32[]{:S(2)}) %collective-permute-start.1) | collective-permute-done | bytes 1048608 | tf_op jit(solution)/shard_map/ppermute | solution.py:21
  40.1 40.0 %collective-permute-done = bf16[2,1024,2,128]{3,2,1,0:T(2,128)(2,1)} collective-permute-done((bf16[2,1024,2,128]{3,2,1,0:T(2,128)(2,1)S(1)}, bf16[2,1024,2,128]{3,2,1,0:T(2,128)(2,1)}, u32[]{:S(2)}, u32[]{:S(2)}) %collective-permute-start) | collective-permute-done | bytes 1048608 | tf_op jit(solution)/shard_map/ppermute | solution.py:18
  80.1 22.7 %pad_maximum_fusion = bf16[2,3072,2,128]{3,2,1,0:T(2,128)(2,1)} fusion(bf16[2,1024,2,128]{3,2,1,0:T(2,128)(2,1)} %collective-permute-done.1, bf16[1,1024,2,128]{3,2,1,0:T(2,128)(2,1)S(1)} %bitcast.159, bf16[1,1024,2,128]{3,2,1,0:T(2,128)(2,1)S(1)} %bitcast.161, bf16[2,1024,2,128]{3,2,1,0:T(2,128)(2,1)} %collective-permute-done), kind=kLoop, calls=%fused_computation.41 | loop fusion | flops 4718592 | bytes 6291456 | tf_op jit(solution)/shard_map/concatenate | solution.py:22
  106.4 272.0 %while.12 = (s32[]{:T(128)}, f32[2,24,128,2,128]{4,2,3,1,0:T(8,128)}, bf16[2,4,128,2,128]{4,2,1,0,3:T(8,128)(2,1)}, s32[2,4,12]{2,1,0:T(4,128)S(1)}, bf16[2,4,12...) while((s32[]{:T(128)}, ...), condition=%wide.region_5.6_spmd, body=%wide.region_1.5_spmd.sunk | while | flops 2440168960 | bytes 288409600 | solution.py:140
  113.7 8.4 %gather_fusion = bf16[48,128,2,128]{3,2,1,0:T(2,128)(2,1)} fusion(bf16[24,128,2,128]{3,2,1,0:T(2,128)(2,1)S(1)} %get-tuple-element.168, s32[1024]{0:T(1024)S(1)} %pad_clamp_fusion.2), kind=kCustom, calls=%fused_computation.clone.1 | custom fusion | bytes 6291648 | tf_op jit(solution)/shard_map/while/body/eval_jaxpr/gather | solution.py:51
  129.2 11.0 %gather_fusion.1 = bf16[48,128,2,128]{3,2,1,0:T(2,128)(2,1)} fusion(bf16[24,128,2,128]{3,2,1,0:T(2,128)(2,1)} %get-tuple-element.171, s32[1024]{0:T(1024)S(1)} %pad_clamp_fusion.2), kind=kCustom, calls=%fused_computation.1.clone.1 | custom fusion | bytes 6291648 | tf_op jit(solution)/shard_map/while/body/eval_jaxpr/gather | solution.py:52
  140.2 8.6 %copy.161 = bf16[4,1536,2,128]{1,3,2,0:T(8,128)(2,1)} copy(bf16[4,1536,2,128]{3,2,1,0:T(2,128)(2,1)} %bitcast.149) | data formatting | bytes 6291456 | tf_op jit(solution)/shard_map/while/body/eval_jaxpr/reshape | solution.py:55
  191.7 11.3 %maximum_bitcast_fusion.2 = f32[4,12,2,128,2,128]{5,3,1,4,0,2:T(8,128)} fusion(f32[1,4,12,128,2,128]{5,3,2,4,1,0:T(8,128)} %bitcast.148, f32[1,4,12,128,2,128]{5,3,2,4,1,0:T(8,128)} %bitcast.147), kind=kLoop, calls=%fused_computation.4.clone.1 | loop fusion | flops 3145728 | bytes 25165824 | tf_op jit(solution)/shard_map/while/body/eval_jaxpr/stack | solution.py:134
  203.0 11.2 %copy.164 = f32[4,12,2,128,2,128]{5,3,4,2,1,0:T(8,128)} copy(f32[4,12,2,128,2,128]{5,3,1,4,0,2:T(8,128)} %maximum_bitcast_fusion.2) | data formatting | bytes 25165824 | tf_op jit(solution)/shard_map/while/body/eval_jaxpr/stack | solution.py:134
  214.3 28.1 %scatter_fusion = f32[2,24,128,2,128]{4,2,3,1,0:T(8,128)} fusion(f32[2,24,128,2,128]{4,2,3,1,0:T(8,128)} %get-tuple-element.182, s32[48]{0:T(128)S(1)} %reshape.231, f32[48,2,128,2,128]{4,2,3,1,0:T(8,128)} %bitcast.146), kind=kCustom, calls=%fused_computation.2.clone.1 | custom fusion | flops 3145728 | bytes 37748928 | tf_op jit(solution)/shard_map/while/body/eval_jaxpr/scatter-add | solution.py:137
  249.7 8.4 %gather_fusion = bf16[48,128,2,128]{3,2,1,0:T(2,128)(2,1)} fusion(bf16[24,128,2,128]{3,2,1,0:T(2,128)(2,1)S(1)} %get-tuple-element.168, s32[1024]{0:T(1024)S(1)} %pad_clamp_fusion.2), kind=kCustom, calls=%fused_computation.clone.1 | custom fusion | bytes 6291648 | tf_op jit(solution)/shard_map/while/body/eval_jaxpr/gather | solution.py:51
  265.1 11.0 %gather_fusion.1 = bf16[48,128,2,128]{3,2,1,0:T(2,128)(2,1)} fusion(bf16[24,128,2,128]{3,2,1,0:T(2,128)(2,1)} %get-tuple-element.171, s32[1024]{0:T(1024)S(1)} %pad_clamp_fusion.2), kind=kCustom, calls=%fused_computation.1.clone.1 | custom fusion | bytes 6291648 | tf_op jit(solution)/shard_map/while/body/eval_jaxpr/gather | solution.py:52
  276.1 8.6 %copy.161 = bf16[4,1536,2,128]{1,3,2,0:T(8,128)(2,1)} copy(bf16[4,1536,2,128]{3,2,1,0:T(2,128)(2,1)} %bitcast.149) | data formatting | bytes 6291456 | tf_op jit(solution)/shard_map/while/body/eval_jaxpr/reshape | solution.py:55
  327.6 11.3 %maximum_bitcast_fusion.2 = f32[4,12,2,128,2,128]{5,3,1,4,0,2:T(8,128)} fusion(f32[1,4,12,128,2,128]{5,3,2,4,1,0:T(8,128)} %bitcast.148, f32[1,4,12,128,2,128]{5,3,2,4,1,0:T(8,128)} %bitcast.147), kind=kLoop, calls=%fused_computation.4.clone.1 | loop fusion | flops 3145728 | bytes 25165824 | tf_op jit(solution)/shard_map/while/body/eval_jaxpr/stack | solution.py:134
  339.0 11.2 %copy.164 = f32[4,12,2,128,2,128]{5,3,4,2,1,0:T(8,128)} copy(f32[4,12,2,128,2,128]{5,3,1,4,0,2:T(8,128)} %maximum_bitcast_fusion.2) | data formatting | bytes 25165824 | tf_op jit(solution)/shard_map/while/body/eval_jaxpr/stack | solution.py:134
  350.2 28.1 %scatter_fusion = f32[2,24,128,2,128]{4,2,3,1,0:T(8,128)} fusion(f32[2,24,128,2,128]{4,2,3,1,0:T(8,128)} %get-tuple-element.182, s32[48]{0:T(128)S(1)} %reshape.231, f32[48,2,128,2,128]{4,2,3,1,0:T(8,128)} %bitcast.146), kind=kCustom, calls=%fused_computation.2.clone.1 | custom fusion | flops 3145728 | bytes 37748928 | tf_op jit(solution)/shard_map/while/body/eval_jaxpr/scatter-add | solution.py:137
  392.7 11.0 %all-to-all-start.1 = ((bf16[1024,2,128]{2,1,0:T(2,128)(2,1)}), bf16[1024,2,128]{2,1,0:T(2,128)(2,1)S(1)}, u32[]{:S(2)}, u32[]{:S(2)}) async-start(bf16[1024,2,128]{2,1,0:T(2,128)(2,1)} %copy.92), calls=%async_computation.1 | async-start | bytes 1048576 | tf_op jit(solution)/shard_map/all_to_all | solution.py:149
  403.7 94.2 %collective-permute-done.2 = f32[2,1024,2,128]{3,1,2,0:T(8,128)S(1)} collective-permute-done((f32[2,1024,2,128]{3,1,2,0:T(8,128)}, f32[2,1024,2,128]{3,1,2,0:T(8,128)S(1)}, u32[]{:S(2)}, u32[]{:S(2)}) %collective-permute-start.2) | collective-permute-done | bytes 2097184 | tf_op jit(solution)/shard_map/ppermute | solution.py:29
  497.9 31.2 %collective-permute-done.3 = f32[2,1024,2,128]{3,1,2,0:T(8,128)} collective-permute-done((f32[2,1024,2,128]{3,1,2,0:T(8,128)}, f32[2,1024,2,128]{3,1,2,0:T(8,128)}, u32[]{:S(2)}, u32[]{:S(2)}) %collective-permute-start.3) | collective-permute-done | bytes 2097184 | tf_op jit(solution)/shard_map/ppermute | solution.py:29
  533.0 10.9 %all-to-all-start.3 = ((bf16[1024,2,128]{2,1,0:T(2,128)(2,1)}), bf16[1024,2,128]{2,1,0:T(2,128)(2,1)S(1)}, u32[]{:S(2)}, u32[]{:S(2)}) async-start(bf16[1024,2,128]{2,1,0:T(2,128)(2,1)} %copy.99), calls=%async_computation.3 | async-start | bytes 1048576 | tf_op jit(solution)/shard_map/all_to_all | solution.py:151
  545.3 18.3 %all-to-all-done.3 = bf16[1024,2,128]{2,1,0:T(2,128)(2,1)S(1)} async-done(((bf16[1024,2,128]{2,1,0:T(2,128)(2,1)}), bf16[1024,2,128]{2,1,0:T(2,128)(2,1)S(1)}, u32[]{:S(2)}, u32[]{:S(2)}) %all-to-all-start.3) | async-done | bytes 524320 | tf_op jit(solution)/shard_map/all_to_all | solution.py:151
  573.4 17.1 %all-to-all-done.2 = bf16[1024,2,128]{2,1,0:T(2,128)(2,1)S(1)} async-done(((bf16[1024,2,128]{2,1,0:T(2,128)(2,1)}), bf16[1024,2,128]{2,1,0:T(2,128)(2,1)S(1)}, u32[]{:S(2)}, u32[]{:S(2)}) %all-to-all-start.2) | async-done | bytes 524320 | tf_op jit(solution)/shard_map/all_to_all | solution.py:150
  (129 shorter events, 155.7 us)
Async XLA Ops:
  0.6 79.5 %copy-start.8 = (bf16[1024,2,128]{2,1,0:T(2,128)(2,1)S(1)}, bf16[1024,2,128]{2,1,0:T(2,128)(2,1)}, u32[]{:S(2)}) copy-start(bf16[1024,2,128]{2,1,0:T(2,128)(2,1)} %param.10) | copy-start | bytes 1572868
  0.6 79.5 %copy-start.9 = (bf16[1024,2,128]{2,1,0:T(2,128)(2,1)S(1)}, bf16[1024,2,128]{2,1,0:T(2,128)(2,1)}, u32[]{:S(2)}) copy-start(bf16[1024,2,128]{2,1,0:T(2,128)(2,1)} %param.9) | copy-start | bytes 1572868
  0.7 30.1 %copy-start.11 = (s32[256]{0:T(256)S(1)}, s32[256]{0:T(256)}, u32[]{:S(2)}) copy-start(s32[256]{0:T(256)} %param.12) | copy-start | bytes 3076
  0.7 30.3 %copy-start.12 = (s32[32]{0:T(128)S(1)}, s32[32]{0:T(128)}, u32[]{:S(2)}) copy-start(s32[32]{0:T(128)} %param.13) | copy-start | bytes 388
  3.5 36.6 %collective-permute-start.1 = (bf16[2,1024,2,128]{3,2,1,0:T(2,128)(2,1)S(1)}, bf16[2,1024,2,128]{3,2,1,0:T(2,128)(2,1)}, u32[]{:S(2)}, u32[]{:S(2)}) collective-permute-start(bf16[2,1024,2,128]{3,2,1,0:T(2,128)(2,1)S(1)} %pad_maximum_fusion.1), channel_id=1, source_target_pairs={{16,0},{32,16},{48,32},{64,48},{80,64},{96,80},{112,96},{128,112},... | collective-permute-start | bytes 3145736 | tf_op jit(solution)/shard_map/ppermute | solution.py:21
  16.6 63.6 %collective-permute-start = (bf16[2,1024,2,128]{3,2,1,0:T(2,128)(2,1)S(1)}, bf16[2,1024,2,128]{3,2,1,0:T(2,128)(2,1)}, u32[]{:S(2)}, u32[]{:S(2)}) collective-permute-start(bf16[2,1024,2,128]{3,2,1,0:T(2,128)(2,1)S(1)} %pad_maximum_fusion.1), channel_id=1, source_target_pairs={{0,16},{16,32},{32,48},{48,64},{64,80},{80,96},{96,112},{112,128},... | collective-permute-start | bytes 3145736 | tf_op jit(solution)/shard_map/ppermute | solution.py:18
  20.6 82.3 %all-to-all-start = ((bf16[64,32,128]{2,0,1:T(8,128)(2,1)}), bf16[64,32,128]{2,0,1:T(8,128)(2,1)S(1)}, u32[]{:S(2)}, u32[]{:S(2)}) async-start(bf16[64,32,128]{2,0,1:T(8,128)(2,1)} %copy.87), calls=%async_computation | async-start | bytes 1048576 | tf_op jit(solution)/shard_map/all_to_all | solution.py:102
  129.2 19.6 %copy-start = (bf16[4,1536,2,128]{1,3,2,0:T(8,128)(2,1)}, bf16[4,1536,2,128]{1,3,2,0:T(8,128)(2,1)S(1)}, u32[]{:S(2)}) copy-start(bf16[4,1536,2,128]{1,3,2,0:T(8,128)(2,1)S(1)} %copy.159) | copy-start | bytes 9437188 | tf_op jit(solution)/shard_map/while
  153.5 3.8 copy-start.4
  153.5 5.1 slice-start
  159.4 3.8 copy-start.1
  214.3 28.1 %copy-start.7 = (bf16[2,4,128,2,128]{4,2,1,0,3:T(8,128)(2,1)S(1)}, bf16[2,4,128,2,128]{4,2,1,0,3:T(8,128)(2,1)}, u32[]{:S(2)}) copy-start(bf16[2,4,128,2,128]{4,2,1,0,3:T(8,128)(2,1)} %copy-done.6) | copy-start | bytes 1572868 | tf_op jit(solution)/shard_map/while
  265.1 19.6 %copy-start = (bf16[4,1536,2,128]{1,3,2,0:T(8,128)(2,1)}, bf16[4,1536,2,128]{1,3,2,0:T(8,128)(2,1)S(1)}, u32[]{:S(2)}) copy-start(bf16[4,1536,2,128]{1,3,2,0:T(8,128)(2,1)S(1)} %copy.159) | copy-start | bytes 9437188 | tf_op jit(solution)/shard_map/while
  289.5 3.8 copy-start.4
  289.5 5.1 slice-start
  295.4 3.8 copy-start.1
  350.2 28.1 %copy-start.7 = (bf16[2,4,128,2,128]{4,2,1,0,3:T(8,128)(2,1)S(1)}, bf16[2,4,128,2,128]{4,2,1,0,3:T(8,128)(2,1)}, u32[]{:S(2)}) copy-start(bf16[2,4,128,2,128]{4,2,1,0,3:T(8,128)(2,1)} %copy-done.6) | copy-start | bytes 1572868 | tf_op jit(solution)/shard_map/while
  381.6 3.9 copy-start.5
  381.6 9.8 %copy-start.10 = (bf16[2,4,128,2,128]{4,2,1,0,3:T(8,128)(2,1)S(1)}, bf16[2,4,128,2,128]{4,2,1,0,3:T(8,128)(2,1)}, u32[]{:S(2)}) copy-start(bf16[2,4,128,2,128]{4,2,1,0,3:T(8,128)(2,1)} %get-tuple-element.46) | copy-start | bytes 1572868
  385.5 112.4 %collective-permute-start.2 = (f32[2,1024,2,128]{3,1,2,0:T(8,128)}, f32[2,1024,2,128]{3,1,2,0:T(8,128)S(1)}, u32[]{:S(2)}, u32[]{:S(2)}) collective-permute-start(f32[2,1024,2,128]{3,1,2,0:T(8,128)} %get-tuple-element.109), channel_id=1, source_target_pairs={{16,0},{32,16},{48,32},{64,48},{80,64},{96,80},{112,96},{128,112},... | collective-permute-start | bytes 6291464 | tf_op jit(solution)/shard_map/ppermute | solution.py:29
  387.4 141.7 %collective-permute-start.3 = (f32[2,1024,2,128]{3,1,2,0:T(8,128)}, f32[2,1024,2,128]{3,1,2,0:T(8,128)}, u32[]{:S(2)}, u32[]{:S(2)}) collective-permute-start(f32[2,1024,2,128]{3,1,2,0:T(8,128)} %get-tuple-element.110), channel_id=1, source_target_pairs={{0,16},{16,32},{32,48},{48,64},{64,80},{80,96},{96,112},{112,128},... | collective-permute-start | bytes 6291464 | tf_op jit(solution)/shard_map/ppermute | solution.py:29
  392.7 140.3 %all-to-all-start.1 = ((bf16[1024,2,128]{2,1,0:T(2,128)(2,1)}), bf16[1024,2,128]{2,1,0:T(2,128)(2,1)S(1)}, u32[]{:S(2)}, u32[]{:S(2)}) async-start(bf16[1024,2,128]{2,1,0:T(2,128)(2,1)} %copy.92), calls=%async_computation.1 | async-start | bytes 1048576 | tf_op jit(solution)/shard_map/all_to_all | solution.py:149
  533.0 30.6 %all-to-all-start.3 = ((bf16[1024,2,128]{2,1,0:T(2,128)(2,1)}), bf16[1024,2,128]{2,1,0:T(2,128)(2,1)S(1)}, u32[]{:S(2)}, u32[]{:S(2)}) async-start(bf16[1024,2,128]{2,1,0:T(2,128)(2,1)} %copy.99), calls=%async_computation.3 | async-start | bytes 1048576 | tf_op jit(solution)/shard_map/all_to_all | solution.py:151
  563.6 26.8 %all-to-all-start.2 = ((bf16[1024,2,128]{2,1,0:T(2,128)(2,1)}), bf16[1024,2,128]{2,1,0:T(2,128)(2,1)S(1)}, u32[]{:S(2)}, u32[]{:S(2)}) async-start(bf16[1024,2,128]{2,1,0:T(2,128)(2,1)} %copy.96), calls=%async_computation.2 | async-start | bytes 1048576 | tf_op jit(solution)/shard_map/all_to_all | solution.py:150
  (8 other events, 17.9 us)
where the time goes:
time: 594 us; the launch traced here: 592 us
  waiting for transfers between devices  210 us (35%)
  local copies, waits for them, and re-layouts  166 us (28%)
  other arithmetic  115 us (19%)
  starting transfers between devices  60.1 us (10%)
  matrix products  39.5 us (7%)
    ppermute x2, waiting for transfers between devices, from_behind(): lax.ppermute(value, axis, [(source, source + steps) for source in range(l...  125 us
    scatter-add x2, other arithmetic, row_step(): return (partial_value.at[:, block_tiles].add(both_grads), query_grad)  56.2 us
    ppermute x1, waiting for transfers between devices, padded(): lax.ppermute(lax.slice_in_dim(block, block.shape[dim] - width, None, axis...  40 us
    concatenate x1, other arithmetic, padded(): block = jnp.concatenate([low, block, high], axis=dim)  22.7 us
    another operation x2, other arithmetic, row_step(): jnp.stack([key_grad, value_grad])  22.7 us
    another operation x2, local copies, waits for them, and re-layouts, row_step(): jnp.stack([key_grad, value_grad])  22.5 us
    gather x2, local copies, waits for them, and re-layouts, pick_keys(): value_sel = tile_array[1][key_tiles]  22 us
    all_to_all x1, waiting for transfers between devices, on_device(): lax.all_to_all(value_grad, 'row', split_axis=0, concat_axis=1, tiled=True)  18.3 us
  transfers between devices with their start and end apart: 8, of which 6 were waited for; matrix products, arithmetic and copies ran while one was open for 6% of the time, Pallas kernels for 0%

commit v1 on v0

v1 whole, which is shorter than its diff:
```python
import functools

import jax
import jax.numpy as jnp
from jax import lax
from jax.experimental import pallas as pl
from jax.experimental.pallas import tpu as pltpu
from jax.sharding import PartitionSpec as P

TILE = 128
GH = 2
GW = 4
WIN_COLS = 2
TPS = 8
NEG = -1e30
LOG2E = 1.4426950408889634


def attend_kernel(
    inv_root, cols_ref, counts_ref, q_ref, g_ref, own_ref, low_ref, high_ref,
    dq_ref, down_ref, dlow_ref, dhigh_ref, acc_ref,
):
    heads, tok_slab, _ = q_ref.shape
    span = WIN_COLS * TILE
    row_len = GW * TILE
    acc_ref[...] = jnp.zeros_like(acc_ref)
    sources = (low_ref, own_ref, high_ref)
    nt = (((1,), (1,)), ((), ()))
    tn = (((0,), (0,)), ((), ()))

    def step(index, carry):
        head = index // TPS
        tile = index % TPS
        rows = pl.ds(pl.multiple_of(tile * TILE, TILE), TILE)
        first = cols_ref[tile]
        query = q_ref[head, rows, :]
        grad = g_ref[head, rows, :]
        starts = []
        keys = []
        values = []
        bias = []
        for slab in range(3):
            for row in range(GH):
                start = pl.multiple_of(row * row_len + first * TILE, TILE)
                starts.append((slab, start))
                keys.append(sources[slab][0, head, pl.ds(start, span), :])
                values.append(sources[slab][1, head, pl.ds(start, span), :])
                for col in range(WIN_COLS):
                    valid = row * GW + first + col < counts_ref[slab]
                    bias.append(jnp.full((TILE, TILE), jnp.where(valid, 0.0, NEG), jnp.float32))
        keys = jnp.concatenate(keys, axis=0)
        values = jnp.concatenate(values, axis=0)
        bias = jnp.concatenate(bias, axis=0)
        scores = lax.dot_general(keys, query, nt, preferred_element_type=jnp.float32)
        scores = scores * (inv_root * LOG2E) + bias
        peak = jnp.max(scores, axis=0, keepdims=True)
        expo = jnp.exp2(scores - peak)
        total = jnp.sum(expo, axis=0, keepdims=True)
        attend = expo * (1.0 / total)
        attend_b = attend.astype(jnp.bfloat16)
        grad_attend = lax.dot_general(values, grad, nt, preferred_element_type=jnp.float32)
        delta = jnp.sum(attend_b.astype(jnp.float32) * grad_attend, axis=0, keepdims=True)
        grad_scores = (attend * (grad_attend - delta)).astype(jnp.bfloat16)
        dq = lax.dot_general(grad_scores, keys, tn, preferred_element_type=jnp.float32)
        dq_ref[head, rows, :] = (dq * inv_root).astype(dq_ref.dtype)
        dk = jnp.dot(grad_scores, query, preferred_element_type=jnp.float32)
        dv = jnp.dot(attend_b, grad, preferred_element_type=jnp.float32)
        for n, (slab, start) in enumerate(starts):
            acc_ref[0, head, slab, pl.ds(start, span), :] += dk[n * span : (n + 1) * span]
            acc_ref[1, head, slab, pl.ds(start, span), :] += dv[n * span : (n + 1) * span]
        return carry

    lax.fori_loop(0, heads * TPS, step, 0)
    for kv, scale in ((0, inv_root), (1, 1.0)):
        for head in range(heads):
            dlow_ref[kv, head] = (acc_ref[kv, head, 0] * scale).astype(dlow_ref.dtype)
            down_ref[kv, head] = acc_ref[kv, head, 1] * scale
            dhigh_ref[kv, head] = (acc_ref[kv, head, 2] * scale).astype(dhigh_ref.dtype)


def attend_call(cols, counts, query, grad, own, low, high):
    heads, tok_slab, head_dim = query.shape
    smem = pl.BlockSpec(memory_space=pltpu.SMEM)
    vmem = pl.BlockSpec(memory_space=pltpu.VMEM)
    pairs = heads * TPS * TILE * 3 * GH * WIN_COLS * TILE
    return pl.pallas_call(
        functools.partial(attend_kernel, head_dim ** (-0.5)),
        out_shape=(
            jax.ShapeDtypeStruct(query.shape, jnp.bfloat16),
            jax.ShapeDtypeStruct(own.shape, jnp.float32),
            jax.ShapeDtypeStruct(own.shape, jnp.bfloat16),
            jax.ShapeDtypeStruct(own.shape, jnp.bfloat16),
        ),
        in_specs=[smem, smem] + [vmem] * 5,
        out_specs=(vmem,) * 4,
        scratch_shapes=[pltpu.VMEM((2, heads, 3, tok_slab, head_dim), jnp.float32)],
        compiler_params=pltpu.CompilerParams(vmem_limit_bytes=48 * 2**20),
        cost_estimate=pl.CostEstimate(
            flops=10 * pairs * head_dim, bytes_accessed=8 * 2**20, transcendentals=pairs
        ),
    )(cols, counts, query, grad, own, low, high)


def on_device(queries, keys, values, out_grad, col_start, valid_tiles):
    slab_total = valid_tiles.shape[0]
    slab_pos = lax.axis_index("slab")
    forward = [(i, i + 1) for i in range(slab_total - 1)]
    backward = [(i + 1, i) for i in range(slab_total - 1)]
    grad = lax.all_to_all(out_grad, "row", split_axis=1, concat_axis=0, tiled=True)
    own = jnp.stack([keys, values]).swapaxes(1, 2)
    low = lax.ppermute(own, "slab", forward)
    high = lax.ppermute(own, "slab", backward)
    cols = lax.dynamic_slice_in_dim(col_start, slab_pos * TPS, TPS, 0)
    padded = jnp.pad(valid_tiles, 1)
    counts = lax.dynamic_slice_in_dim(padded, slab_pos, 3, 0)
    dq, down, dlow, dhigh = attend_call(
        cols, counts, queries.swapaxes(0, 1), grad.swapaxes(0, 1), own, low, high
    )
    from_high = lax.ppermute(dlow, "slab", backward)
    from_low = lax.ppermute(dhigh, "slab", forward)
    sums = down + from_high.astype(jnp.float32) + from_low.astype(jnp.float32)
    sums = sums.astype(jnp.bfloat16)

    def home(array):
        return lax.all_to_all(array.swapaxes(0, 1), "row", split_axis=0, concat_axis=1, tiled=True)

    return home(dq), home(sums[0]), home(sums[1])


def solution(mesh):
    head_split = P("slab", "row", None)
    token_split = P(("slab", "row"), None, None)
    return jax.shard_map(
        on_device,
        mesh=mesh,
        in_specs=(head_split, head_split, head_split, token_split, P(), P()),
        out_specs=(token_split,) * 3,
        check_vma=False,
    )
```

time: 594 us -> 286 us (0.48)
  the two profiles are of different devices: /device:TPU:8 before, /device:TPU:41 now
where the time goes in v1:
time: 286 us; the launch traced here: 285 us
  waiting for transfers between devices  187 us (65%)
  starting transfers between devices  56.6 us (20%)
  Pallas kernels  25.4 us (9%)
  local copies, waits for them, and re-layouts  13.1 us (5%)
    all_to_all x3, waiting for transfers between devices, home(): lax.all_to_all(array.swapaxes(0, 1), 'row', split_axis=0, concat_axis=1,...  59.9 us
    ppermute x1, waiting for transfers between devices, on_device(): from_high = lax.ppermute(dlow, 'slab', backward)  40 us
    all_to_all x1, waiting for transfers between devices, on_device(): lax.all_to_all(out_grad, 'row', split_axis=1, concat_axis=0, tiled=True)  28.7 us
    all_to_all x3, starting transfers between devices, home(): lax.all_to_all(array.swapaxes(0, 1), 'row', split_axis=0, concat_axis=1,...  25.6 us
    pallas_call x1, Pallas kernels, attend_call(): pl.pallas_call(functools.partial(attend_kernel, head_dim ** (-0.5)), out_...  25.4 us
    ppermute x1, waiting for transfers between devices, on_device(): from_low = lax.ppermute(dhigh, 'slab', forward)  24.9 us
    ppermute x1, waiting for transfers between devices, on_device(): low = lax.ppermute(own, 'slab', forward)  21.8 us
    all_to_all x1, starting transfers between devices, on_device(): lax.all_to_all(out_grad, 'row', split_axis=1, concat_axis=0, tiled=True)  17.3 us
  transfers between devices with their start and end apart: 8, of which 7 were waited for; matrix products, arithmetic and copies ran while one was open for 3% of the time, Pallas kernels for 0%

profile of v1, /device:TPU:41, one launch (start us, length us, event | category | flops | bytes accessed | tf_op | source)
XLA Modules:
  0.0 285.3 jit_solution(11957704412570286148)
XLA Ops:
  0.7 2.1 copy.17
  2.8 17.3 %all-to-all-start = ((bf16[64,32,128]{2,0,1:T(8,128)(2,1)}), bf16[64,32,128]{2,0,1:T(8,128)(2,1)S(1)}, u32[]{:S(2)}, u32[]{:S(2)}) async-start(bf16[64,32,128]{2,0,1:T(8,128)(2,1)} %copy.17), calls=%async_computation | async-start | bytes 1048576 | tf_op jit(solution)/shard_map/all_to_all | solution.py:109
  20.4 2.7 collective-permute-start.1
  23.1 2.6 collective-permute-start
  27.0 28.7 %all-to-all-done = bf16[64,32,128]{2,0,1:T(8,128)(2,1)S(1)} async-done(((bf16[64,32,128]{2,0,1:T(8,128)(2,1)}), bf16[64,32,128]{2,0,1:T(8,128)(2,1)S(1)}, u32[]{:S(2)}, u32[]{:S(2)}) %all-to-all-start) | async-done | bytes 524320 | tf_op jit(solution)/shard_map/all_to_all | solution.py:109
  55.7 12.1 %collective-permute-done.1.high_ref = bf16[2,2,1024,128]{3,2,1,0:T(8,128)(2,1)} collective-permute-done((bf16[2,2,1024,128]{3,2,1,0:T(8,128)(2,1)S(1)}, bf16[2,2,1024,128]{3,2,1,0:T(8,128)(2,1)}, u32[]{:S(2)}, u32[]{:S(2)}) %collective-permute-start.1) | collective-permute-done | bytes 1048608 | tf_op jit(solution)/shard_map/ppermute | solution.py:112
  67.8 21.8 %collective-permute-done.low_ref = bf16[2,2,1024,128]{3,2,1,0:T(8,128)(2,1)S(1)} collective-permute-done((bf16[2,2,1024,128]{3,2,1,0:T(8,128)(2,1)S(1)}, bf16[2,2,1024,128]{3,2,1,0:T(8,128)(2,1)S(1)}, u32[]{:S(2)}, u32[]{:S(2)}) %collective-permute-start) | collective-permute-done | bytes 1048608 | tf_op jit(solution)/shard_map/ppermute | solution.py:111
  89.6 25.4 %shard_map.85 = (bf16[2,1024,128]{2,1,0:T(8,128)(2,1)S(1)}, f32[2,2,1024,128]{3,2,1,0:T(8,128)}, bf16[2,2,1024,128]{3,2,1,0:T(8,128)(2,1)S(1)}, bf16[2,2,1024,128]{3,2,1,0:T(8,128)(2,1)S(1)}) custom-call(s32[8]{0:T(128)S(1)} %dynamic_slice.6.cols_ref, s32[3]{0:T(128)S(1)} %pad_dynamic-slice_fusion.counts_ref, bf16[2,1024,128]{2,1,0:T(8,128)(2,1)S(1)} %bitcast.36, ...), custom_call_target="tpu_custom_call" | custom-call | flops 4026531840 | bytes 8388608 | tf_op jit(solution)/shard_map/pallas_call | solution.py:86
  117.0 1.3 copy.21
  118.3 10.8 %all-to-all-start.1 = ((bf16[1024,2,128]{2,1,0:T(2,128)(2,1)}), bf16[1024,2,128]{2,1,0:T(2,128)(2,1)S(1)}, u32[]{:S(2)}, u32[]{:S(2)}) async-start(bf16[1024,2,128]{2,1,0:T(2,128)(2,1)} %copy.21), calls=%async_computation.1 | async-start | bytes 1048576 | tf_op jit(solution)/shard_map/all_to_all | solution.py:125
  129.1 6.4 %collective-permute-start.2 = (bf16[2,2,1024,128]{3,2,1,0:T(8,128)(2,1)S(1)}, bf16[2,2,1024,128]{3,2,1,0:T(8,128)(2,1)S(1)}, u32[]{:S(2)}, u32[]{:S(2)}) collective-permute-start(bf16[2,2,1024,128]{3,2,1,0:T(8,128)(2,1)S(1)} %copy-done.3), channel_id=1, source_target_pairs={{16,0},{32,16},{48,32},{64,48},{80,64},{96,80},{112,96},{128,112},... | collective-permute-start | bytes 3145736 | tf_op jit(solution)/shard_map/ppermute | solution.py:119
  135.5 1.9 collective-permute-start.3
  137.5 40.0 %collective-permute-done.2 = bf16[2,2,1024,128]{3,2,1,0:T(8,128)(2,1)S(1)} collective-permute-done((bf16[2,2,1024,128]{3,2,1,0:T(8,128)(2,1)S(1)}, bf16[2,2,1024,128]{3,2,1,0:T(8,128)(2,1)S(1)}, u32[]{:S(2)}, u32[]{:S(2)}) %collective-permute-start.2) | collective-permute-done | bytes 1048608 | tf_op jit(solution)/shard_map/ppermute | solution.py:119
  177.5 24.9 %collective-permute-done.3 = bf16[2,2,1024,128]{3,2,1,0:T(8,128)(2,1)S(1)} collective-permute-done((bf16[2,2,1024,128]{3,2,1,0:T(8,128)(2,1)S(1)}, bf16[2,2,1024,128]{3,2,1,0:T(8,128)(2,1)S(1)}, u32[]{:S(2)}, u32[]{:S(2)}) %collective-permute-start.3) | collective-permute-done | bytes 1048608 | tf_op jit(solution)/shard_map/ppermute | solution.py:120
  202.4 2.0 add_convert_fusion
  204.5 1.3 copy.25
  205.8 10.3 %all-to-all-start.3 = ((bf16[1024,2,128]{2,1,0:T(2,128)(2,1)}), bf16[1024,2,128]{2,1,0:T(2,128)(2,1)S(1)}, u32[]{:S(2)}, u32[]{:S(2)}) async-start(bf16[1024,2,128]{2,1,0:T(2,128)(2,1)} %copy.25), calls=%async_computation.3 | async-start | bytes 1048576 | tf_op jit(solution)/shard_map/all_to_all | solution.py:125
  216.1 1.3 copy.23
  217.4 33.3 %all-to-all-done.3 = bf16[1024,2,128]{2,1,0:T(2,128)(2,1)S(1)} async-done(((bf16[1024,2,128]{2,1,0:T(2,128)(2,1)}), bf16[1024,2,128]{2,1,0:T(2,128)(2,1)S(1)}, u32[]{:S(2)}, u32[]{:S(2)}) %all-to-all-start.3) | async-done | bytes 524320 | tf_op jit(solution)/shard_map/all_to_all | solution.py:125
  250.7 4.5 %all-to-all-start.2 = ((bf16[1024,2,128]{2,1,0:T(2,128)(2,1)}), bf16[1024,2,128]{2,1,0:T(2,128)(2,1)S(1)}, u32[]{:S(2)}, u32[]{:S(2)}) async-start(bf16[1024,2,128]{2,1,0:T(2,128)(2,1)} %copy.23), calls=%async_computation.2 | async-start | bytes 1048576 | tf_op jit(solution)/shard_map/all_to_all | solution.py:125
  255.3 1.2 copy.22
  256.4 1.2 copy.26
  257.6 26.6 %all-to-all-done.2 = bf16[1024,2,128]{2,1,0:T(2,128)(2,1)S(1)} async-done(((bf16[1024,2,128]{2,1,0:T(2,128)(2,1)}), bf16[1024,2,128]{2,1,0:T(2,128)(2,1)S(1)}, u32[]{:S(2)}, u32[]{:S(2)}) %all-to-all-start.2) | async-done | bytes 524320 | tf_op jit(solution)/shard_map/all_to_all | solution.py:125
  284.2 1.2 copy.24
  (24 shorter events, 3.6 us)
Async XLA Ops:
  0.6 19.5 %copy-start.4 = (bf16[1024,2,128]{2,1,0:T(2,128)(2,1)S(1)}, bf16[1024,2,128]{2,1,0:T(2,128)(2,1)}, u32[]{:S(2)}) copy-start(bf16[1024,2,128]{2,1,0:T(2,128)(2,1)} %param.8) | copy-start | bytes 1572868
  0.6 19.5 %copy-start.5 = (bf16[1024,2,128]{2,1,0:T(2,128)(2,1)S(1)}, bf16[1024,2,128]{2,1,0:T(2,128)(2,1)}, u32[]{:S(2)}) copy-start(bf16[1024,2,128]{2,1,0:T(2,128)(2,1)} %param.7) | copy-start | bytes 1572868
  2.8 52.9 %all-to-all-start = ((bf16[64,32,128]{2,0,1:T(8,128)(2,1)}), bf16[64,32,128]{2,0,1:T(8,128)(2,1)S(1)}, u32[]{:S(2)}, u32[]{:S(2)}) async-start(bf16[64,32,128]{2,0,1:T(8,128)(2,1)} %copy.17), calls=%async_computation | async-start | bytes 1048576 | tf_op jit(solution)/shard_map/all_to_all | solution.py:109
  20.3 6.6 %copy-start.6 = (s32[256]{0:T(256)S(1)}, s32[256]{0:T(256)}, u32[]{:S(2)}) copy-start(s32[256]{0:T(256)} %param.10) | copy-start | bytes 3076
  20.3 6.7 %copy-start.7 = (s32[32]{0:T(128)S(1)}, s32[32]{0:T(128)}, u32[]{:S(2)}) copy-start(s32[32]{0:T(128)} %param.11) | copy-start | bytes 388
  20.4 47.4 %collective-permute-start.1 = (bf16[2,2,1024,128]{3,2,1,0:T(8,128)(2,1)S(1)}, bf16[2,2,1024,128]{3,2,1,0:T(8,128)(2,1)}, u32[]{:S(2)}, u32[]{:S(2)}) collective-permute-start(bf16[2,2,1024,128]{3,2,1,0:T(8,128)(2,1)S(1)} %maximum_bitcast_fusion.own_ref), channel_id=1, source_target_pairs={{16,0},{32,16},{48,32},{64,48},{80,64},{96,80},{112,96},{128,112},... | collective-permute-start | bytes 3145736 | tf_op jit(solution)/shard_map/ppermute | solution.py:112
  23.1 66.6 %collective-permute-start = (bf16[2,2,1024,128]{3,2,1,0:T(8,128)(2,1)S(1)}, bf16[2,2,1024,128]{3,2,1,0:T(8,128)(2,1)S(1)}, u32[]{:S(2)}, u32[]{:S(2)}) collective-permute-start(bf16[2,2,1024,128]{3,2,1,0:T(8,128)(2,1)S(1)} %maximum_bitcast_fusion.own_ref), channel_id=1, source_target_pairs={{0,16},{16,32},{32,48},{48,64},{64,80},{80,96},{96,112},{112,128},... | collective-permute-start | bytes 3145736 | tf_op jit(solution)/shard_map/ppermute | solution.py:111
  115.0 1.0 copy-start
  116.0 1.0 copy-start.2
  117.0 12.1 %copy-start.3 = (bf16[2,2,1024,128]{3,2,1,0:T(8,128)(2,1)S(1)}, bf16[2,2,1024,128]{3,2,1,0:T(8,128)(2,1)}, u32[]{:S(2)}) copy-start(bf16[2,2,1024,128]{3,2,1,0:T(8,128)(2,1)} %copy-done.2) | copy-start | bytes 3145732
  117.0 18.6 %copy-start.1 = (bf16[2,2,1024,128]{3,2,1,0:T(8,128)(2,1)S(1)}, bf16[2,2,1024,128]{3,2,1,0:T(8,128)(2,1)}, u32[]{:S(2)}) copy-start(bf16[2,2,1024,128]{3,2,1,0:T(8,128)(2,1)} %copy-done) | copy-start | bytes 3145732
  118.3 87.5 %all-to-all-start.1 = ((bf16[1024,2,128]{2,1,0:T(2,128)(2,1)}), bf16[1024,2,128]{2,1,0:T(2,128)(2,1)S(1)}, u32[]{:S(2)}, u32[]{:S(2)}) async-start(bf16[1024,2,128]{2,1,0:T(2,128)(2,1)} %copy.21), calls=%async_computation.1 | async-start | bytes 1048576 | tf_op jit(solution)/shard_map/all_to_all | solution.py:125
  129.1 48.4 %collective-permute-start.2 = (bf16[2,2,1024,128]{3,2,1,0:T(8,128)(2,1)S(1)}, bf16[2,2,1024,128]{3,2,1,0:T(8,128)(2,1)S(1)}, u32[]{:S(2)}, u32[]{:S(2)}) collective-permute-start(bf16[2,2,1024,128]{3,2,1,0:T(8,128)(2,1)S(1)} %copy-done.3), channel_id=1, source_target_pairs={{16,0},{32,16},{48,32},{64,48},{80,64},{96,80},{112,96},{128,112},... | collective-permute-start | bytes 3145736 | tf_op jit(solution)/shard_map/ppermute | solution.py:119
  135.5 66.9 %collective-permute-start.3 = (bf16[2,2,1024,128]{3,2,1,0:T(8,128)(2,1)S(1)}, bf16[2,2,1024,128]{3,2,1,0:T(8,128)(2,1)S(1)}, u32[]{:S(2)}, u32[]{:S(2)}) collective-permute-start(bf16[2,2,1024,128]{3,2,1,0:T(8,128)(2,1)S(1)} %copy-done.1), channel_id=1, source_target_pairs={{0,16},{16,32},{32,48},{48,64},{64,80},{80,96},{96,112},{112,128},... | collective-permute-start | bytes 3145736 | tf_op jit(solution)/shard_map/ppermute | solution.py:120
  205.8 44.9 %all-to-all-start.3 = ((bf16[1024,2,128]{2,1,0:T(2,128)(2,1)}), bf16[1024,2,128]{2,1,0:T(2,128)(2,1)S(1)}, u32[]{:S(2)}, u32[]{:S(2)}) async-start(bf16[1024,2,128]{2,1,0:T(2,128)(2,1)} %copy.25), calls=%async_computation.3 | async-start | bytes 1048576 | tf_op jit(solution)/shard_map/all_to_all | solution.py:125
  250.7 33.4 %all-to-all-start.2 = ((bf16[1024,2,128]{2,1,0:T(2,128)(2,1)}), bf16[1024,2,128]{2,1,0:T(2,128)(2,1)S(1)}, u32[]{:S(2)}, u32[]{:S(2)}) async-start(bf16[1024,2,128]{2,1,0:T(2,128)(2,1)} %copy.23), calls=%async_computation.2 | async-start | bytes 1048576 | tf_op jit(solution)/shard_map/all_to_all | solution.py:125

commit v2 on v1

v2 whole, which is shorter than its diff:
```python
import functools

import jax
import jax.numpy as jnp
from jax import lax
from jax.experimental import pallas as pl
from jax.experimental.pallas import tpu as pltpu
from jax.sharding import PartitionSpec as P

TILE = 128
GH = 2
GW = 4
WIN_COLS = 2
TPS = 8
NEG = -1e30
LOG2E = 1.4426950408889634
MESH = pl.DeviceIdType.MESH
NT = (((1,), (1,)), ((), ()))
TN = (((0,), (0,)), ((), ()))


def fused_kernel(
    slabs, rows, inv_root, shift_ref, bias_ref, q_ref, k_ref, v_ref, g_ref,
    oq_ref, okv_ref,
    q_side, g_own, g_side, expo_ref, gatt_ref, stat, stat_in, final, final_in,
    acc, kv_out, dq_own, dq_side, dq_in, dq_out,
    q_send, q_recv, a_send, a_recv, g_send, g_recv, s_send, s_recv, f_send, f_recv,
    kv_send, kv_recv, dq_send, dq_recv, o_send, o_recv,
):
    heads, tok_slab, head_dim = q_ref.shape
    block = g_ref.shape[1]
    span = WIN_COLS * TILE
    row_len = GW * TILE
    slab = lax.axis_index("slab")
    row = lax.axis_index("row")
    below = lax.rem(slab + slabs - 1, slabs)
    above = lax.rem(slab + 1, slabs)
    sides = (below, above)

    def peer(step):
        return lax.rem(row + step, rows)

    barrier = pltpu.get_barrier_semaphore()
    for side in sides:
        pl.semaphore_signal(barrier, inc=1, device_id=(side, row), device_id_type=MESH)

    def greet(step, carry):
        pl.semaphore_signal(barrier, inc=1, device_id=(slab, peer(step)), device_id_type=MESH)
        return carry

    lax.fori_loop(1, rows, greet, 0)
    pl.semaphore_wait(barrier, rows + 1)

    def to_side(src, dst, n, send, recv, head):
        return pltpu.make_async_remote_copy(
            src_ref=src,
            dst_ref=dst,
            send_sem=send.at[head, n],
            recv_sem=recv.at[head, 1 - n],
            device_id=(sides[n], row),
            device_id_type=MESH,
        )

    def from_side(ref, n, recv, head):
        pltpu.make_async_copy(ref, ref, recv.at[head, n]).wait()

    def all_sent(ref, sem):
        pltpu.make_async_copy(ref, ref, sem).wait()

    def send_queries(head):
        for n in range(2):
            to_side(q_ref.at[head], q_side.at[1 - n, head], n, q_send, q_recv, head).start()

    def spread_grad(head):
        def one(step, carry):
            other = peer(step)
            pltpu.make_async_remote_copy(
                src_ref=g_ref.at[other * heads + head],
                dst_ref=g_own.at[head, row],
                send_sem=a_send.at[head],
                recv_sem=a_recv.at[head],
                device_id=(slab, other),
                device_id_type=MESH,
            ).start()
            return carry

        lax.fori_loop(1, rows, one, 0)
        g_own[head, row] = g_ref[row * heads + head]

    def await_spread(buffer, send, recv, head):
        whole = buffer.at[pl.ds(0, rows - 1)]
        pltpu.make_async_copy(whole, whole, recv.at[head]).wait()
        pltpu.make_async_copy(whole, whole, send.at[head]).wait()

    def send_grads(head):
        for n in range(2):
            to_side(g_own.at[head], g_side.at[1 - n, head], n, g_send, g_recv, head).start()

    def pick(ref, head, tile, part):
        base = (tile % GW) // 2
        high = jnp.broadcast_to(shift_ref[part, pl.ds(tile, 1), :], (TILE, head_dim))
        high = high.astype(jnp.bfloat16)
        low = 1 - high
        chosen = []
        for r in range(GH):
            cols = [
                ref[head, pl.ds(pl.multiple_of((r * GW + base + c) * TILE, TILE), TILE), :]
                for c in range(WIN_COLS + 1)
            ]
            chosen += [cols[c] * low + cols[c + 1] * high for c in range(WIN_COLS)]
        return jnp.concatenate(chosen, axis=0)

    def query_of(head, tile, part):
        at = pl.ds(pl.multiple_of(tile * TILE, TILE), TILE)
        if part == 1:
            return q_ref[head, at, :]
        return q_side[part // 2, head, at, :]

    def grad_of(head, tile, part):
        each = TILE // block
        at = pl.ds(tile * each, each)
        if part == 1:
            return g_own[head, at].reshape(TILE, head_dim)
        return g_side[part // 2, head, at].reshape(TILE, head_dim)

    def first_pass(head, part):
        def one(tile, carry):
            keys = pick(k_ref, head, tile, part)
            values = pick(v_ref, head, tile, part)
            bias = jnp.concatenate(
                [
                    jnp.broadcast_to(bias_ref[n, part, pl.ds(tile, 1), :], (TILE, TILE))
                    for n in range(GH * WIN_COLS)
                ],
                axis=0,
            )
            scores = lax.dot_general(
                keys, query_of(head, tile, part), NT, preferred_element_type=jnp.float32
            )
            scores = scores * (inv_root * LOG2E) + bias
            peak = jnp.max(scores, axis=0, keepdims=True)
            expo = jnp.exp2(scores - peak)
            grad_attend = lax.dot_general(
                values, grad_of(head, tile, part), NT, preferred_element_type=jnp.float32
            )
            expo_ref[part, tile] = expo
            gatt_ref[part, tile] = grad_attend
            at = pl.ds(tile, 1)
            stat[head, part, 0, at, :] = peak
            stat[head, part, 1, at, :] = jnp.sum(expo, axis=0, keepdims=True)
            stat[head, part, 2, at, :] = jnp.sum(expo * grad_attend, axis=0, keepdims=True)
            return carry

        lax.fori_loop(0, TPS, one, 0)

    def send_stats(head):
        for n in range(2):
            to_side(
                stat.at[head, 2 * n], stat_in.at[1 - n, head], n, s_send, s_recv, head
            ).start()

    def combine(head):
        for n in range(2):
            from_side(stat_in.at[n, head], n, s_recv, head)
        peaks = [stat_in[0, head, 0], stat[head, 1, 0], stat_in[1, head, 0]]
        sums = [stat_in[0, head, 1], stat[head, 1, 1], stat_in[1, head, 1]]
        dots = [stat_in[0, head, 2], stat[head, 1, 2], stat_in[1, head, 2]]
        top = jnp.maximum(jnp.maximum(peaks[0], peaks[1]), peaks[2])
        weights = [jnp.exp2(p - top) for p in peaks]
        total = sum(w * s for w, s in zip(weights, sums))
        final[head, 0] = top
        final[head, 1] = 1.0 / total
        final[head, 2] = sum(w * d for w, d in zip(weights, dots)) / total
        for n in range(2):
            to_side(
                final.at[head], final_in.at[1 - n, head], n, f_send, f_recv, head
            ).start()

    def second_pass(head, part):
        def one(tile, carry):
            base = (tile % GW) // 2
            at = pl.ds(tile, 1)
            shifted = jnp.broadcast_to(shift_ref[part, at, :], (TILE, head_dim)) > 0.5
            keys = pick(k_ref, head, tile, part)
            src = final.at[head] if part == 1 else final_in.at[part // 2, head]
            scale = jnp.exp2(stat[head, part, 0, at, :] - src[0, at, :]) * src[1, at, :]
            attend = expo_ref[part, tile] * scale
            grad_scores = (attend * (gatt_ref[part, tile] - src[2, at, :])).astype(jnp.bfloat16)
            attend_b = attend.astype(jnp.bfloat16)
            dq = lax.dot_general(grad_scores, keys, TN, preferred_element_type=jnp.float32)
            rows_at = pl.ds(pl.multiple_of(tile * TILE, TILE), TILE)
            if part == 1:
                dq_own[rows_at, :] = dq * inv_root
            else:
                dq_side[part // 2, head, rows_at, :] = (dq * inv_root).astype(jnp.bfloat16)
            dk = jnp.dot(
                grad_scores, query_of(head, tile, part), preferred_element_type=jnp.float32
            )
            dv = jnp.dot(
                attend_b, grad_of(head, tile, part), preferred_element_type=jnp.float32
            )
            for which, term in ((0, dk), (1, dv)):
                for r in range(GH):
                    near = term[r * span : r * span + TILE]
                    far = term[r * span + TILE : (r + 1) * span]
                    adds = (
                        jnp.where(shifted, 0.0, near),
                        jnp.where(shifted, near, far),
                        jnp.where(shifted, far, 0.0),
                    )
                    for col, add in enumerate(adds):
                        where = pl.ds(
                            pl.multiple_of((r * GW + base + col) * TILE, TILE), TILE
                        )
                        acc[which, where, :] += add
            return carry

        lax.fori_loop(0, TPS, one, 0)

    def send_home(head):
        def stage(other, carry):
            at = pl.ds(pl.multiple_of(other * block, block), block)
            kv_out[head, other, 0] = (acc[0, at, :] * inv_root).astype(jnp.bfloat16)
            kv_out[head, other, 1] = acc[1, at, :].astype(jnp.bfloat16)
            return carry

        lax.fori_loop(0, rows, stage, 0)

        def one(step, carry):
            other = peer(step)
            pltpu.make_async_remote_copy(
                src_ref=kv_out.at[head, other],
                dst_ref=okv_ref.at[row * heads + head],
                send_sem=kv_send.at[head],
                recv_sem=kv_recv.at[head],
                device_id=(slab, other),
                device_id_type=MESH,
            ).start()
            return carry

        lax.fori_loop(1, rows, one, 0)
        okv_ref[row * heads + head] = kv_out[head, row]

    def send_dq(head):
        for n in range(2):
            to_side(
                dq_side.at[n, head], dq_in.at[1 - n, head], n, dq_send, dq_recv, head
            ).start()

    def finish_dq(head):
        for n in range(2):
            from_side(dq_in.at[n, head], n, dq_recv, head)

        def stage(other, carry):
            at = pl.ds(pl.multiple_of(other * block, block), block)
            total = (
                dq_mid[head][at, :]
                + dq_in[0, head, at, :].astype(jnp.float32)
                + dq_in[1, head, at, :].astype(jnp.float32)
            )
            dq_out[head, other] = total.astype(jnp.bfloat16)
            return carry

        lax.fori_loop(0, rows, stage, 0)

        def one(step, carry):
            other = peer(step)
            pltpu.make_async_remote_copy(
                src_ref=dq_out.at[head, other],
                dst_ref=oq_ref.at[row * heads + head],
                send_sem=o_send.at[head],
                recv_sem=o_recv.at[head],
                device_id=(slab, other),
                device_id_type=MESH,
            ).start()
            return carry

        lax.fori_loop(1, rows, one, 0)
        oq_ref[row * heads + head] = dq_out[head, row]

    dq_all = dq_own
    dq_mid = [dq_all.at[head] for head in range(heads)]

    send_queries(0)
    spread_grad(0)
    for head in range(heads):
        await_spread(g_own.at[head], a_send, a_recv, head)
        send_grads(head)
        if head + 1 < heads:
            spread_grad(head + 1)
            send_queries(head + 1)

    for head in range(heads):
        dq_own = dq_mid[head]
        acc[...] = jnp.zeros_like(acc)
        first_pass(head, 1)
        for n in range(2):
            from_side(q_side.at[n, head], n, q_recv, head)
            from_side(g_side.at[n, head], n, g_recv, head)
            first_pass(head, 2 * n)
        send_stats(head)
        combine(head)
        second_pass(head, 1)
        for n in range(2):
            from_side(final_in.at[n, head], n, f_recv, head)
            second_pass(head, 2 * n)
        send_dq(head)
        send_home(head)
    for head in range(heads):
        finish_dq(head)

    for head in range(heads):
        for n in range(2):
            to_side(q_ref.at[head], q_side.at[1 - n, head], n, q_send, q_recv, head).wait_send()
            to_side(g_own.at[head], g_side.at[1 - n, head], n, g_send, g_recv, head).wait_send()
            to_side(stat.at[head, 2 * n], stat_in.at[1 - n, head], n, s_send, s_recv, head).wait_send()
            to_side(final.at[head], final_in.at[1 - n, head], n, f_send, f_recv, head).wait_send()
            to_side(dq_side.at[n, head], dq_in.at[1 - n, head], n, dq_send, dq_recv, head).wait_send()
        await_spread(kv_out.at[head], kv_send, kv_recv, head)
    for head in range(heads):
        await_spread(dq_out.at[head], o_send, o_recv, head)


def fused_call(shift, bias, query, key, value, grad, slabs, rows):
    heads, tok_slab, head_dim = query.shape
    block = grad.shape[1]
    vmem = pl.BlockSpec(memory_space=pltpu.VMEM)
    keys_seen = GH * WIN_COLS * TILE
    pairs = heads * tok_slab * 3 * keys_seen
    low, full = jnp.bfloat16, jnp.float32
    side = pltpu.VMEM((2, heads, tok_slab, head_dim), low)
    return pl.pallas_call(
        functools.partial(fused_kernel, slabs, rows, head_dim ** (-0.5)),
        out_shape=(
            jax.ShapeDtypeStruct((rows * heads, block, head_dim), low),
            jax.ShapeDtypeStruct((rows * heads, 2, block, head_dim), low),
        ),
        in_specs=[vmem] * 6,
        out_specs=(vmem, vmem),
        scratch_shapes=[
            side,
            pltpu.VMEM((heads, rows, block, head_dim), low),
            pltpu.VMEM((2, heads, rows, block, head_dim), low),
            pltpu.VMEM((3, TPS, keys_seen, TILE), full),
            pltpu.VMEM((3, TPS, keys_seen, TILE), full),
            pltpu.VMEM((heads, 3, 3, TPS, TILE), full),
            pltpu.VMEM((2, heads, 3, TPS, TILE), full),
            pltpu.VMEM((heads, 3, TPS, TILE), full),
            pltpu.VMEM((2, heads, 3, TPS, TILE), full),
            pltpu.VMEM((2, tok_slab, head_dim), full),
            pltpu.VMEM((heads, rows, 2, block, head_dim), low),
            pltpu.VMEM((heads, tok_slab, head_dim), full),
            side,
            side,
            pltpu.VMEM((heads, rows, block, head_dim), low),
        ]
        + [
            pltpu.SemaphoreType.DMA((heads, 2)), pltpu.SemaphoreType.DMA((heads, 2)),
            pltpu.SemaphoreType.DMA((heads,)), pltpu.SemaphoreType.DMA((heads,)),
            pltpu.SemaphoreType.DMA((heads, 2)), pltpu.SemaphoreType.DMA((heads, 2)),
            pltpu.SemaphoreType.DMA((heads, 2)), pltpu.SemaphoreType.DMA((heads, 2)),
            pltpu.SemaphoreType.DMA((heads, 2)), pltpu.SemaphoreType.DMA((heads, 2)),
            pltpu.SemaphoreType.DMA((heads,)), pltpu.SemaphoreType.DMA((heads,)),
            pltpu.SemaphoreType.DMA((heads, 2)), pltpu.SemaphoreType.DMA((heads, 2)),
            pltpu.SemaphoreType.DMA((heads,)), pltpu.SemaphoreType.DMA((heads,)),
        ],
        compiler_params=pltpu.CompilerParams(
            collective_id=0, has_side_effects=True, vmem_limit_bytes=50 * 2**20
        ),
        cost_estimate=pl.CostEstimate(
            flops=10 * pairs * head_dim, bytes_accessed=8 * 2**20, transcendentals=pairs
        ),
    )(shift, bias, query, key, value, grad)


def window_terms(slabs, col_start, valid_tiles):
    slab = lax.axis_index("slab")
    tile = jnp.arange(TPS, dtype=jnp.int32)
    owners = slab + jnp.arange(-1, 2, dtype=jnp.int32)
    inside = (owners >= 0) & (owners < slabs)
    padded = jnp.pad(col_start.reshape(slabs, TPS), ((1, 1), (0, 0)))
    first = lax.dynamic_slice_in_dim(padded, slab, 3, 0)
    shift = first - (tile % GW) // 2
    slot = jnp.arange(GH * WIN_COLS, dtype=jnp.int32)
    inner = (slot // WIN_COLS * GW + slot % WIN_COLS)[:, None, None] + first
    limit = lax.dynamic_index_in_dim(valid_tiles, slab, 0, False)
    bias = jnp.where((inner < limit) & inside[:, None], 0.0, NEG)
    wide = lambda a: jnp.broadcast_to(a.astype(jnp.float32)[..., None], a.shape + (TILE,))
    return wide(shift), wide(bias)


def on_device(slabs, rows, queries, keys, values, out_grad, col_start, valid_tiles):
    shift, bias = window_terms(slabs, col_start, valid_tiles)
    dq, dkv = fused_call(
        shift, bias, queries.swapaxes(0, 1), keys.swapaxes(0, 1),
        values.swapaxes(0, 1), out_grad.swapaxes(0, 1), slabs, rows,
    )
    return dq.swapaxes(0, 1), dkv[:, 0].swapaxes(0, 1), dkv[:, 1].swapaxes(0, 1)


def solution(mesh):
    head_split = P("slab", "row", None)
    token_split = P(("slab", "row"), None, None)
    return jax.shard_map(
        functools.partial(on_device, mesh.shape["slab"], mesh.shape["row"]),
        mesh=mesh,
        in_specs=(head_split, head_split, head_split, token_split, P(), P()),
        out_specs=(token_split,) * 3,
        check_vma=False,
    )
```

time: 286 us -> 223 us (0.78)
  the two profiles are of different devices: /device:TPU:41 before, /device:TPU:1 now
where the time goes in v2:
time: 223 us
  Pallas kernels  214 us (96%)
  local copies, waits for them, and re-layouts  8.12 us (4%)
    pallas_call x1, Pallas kernels, fused_call(): pl.pallas_call(functools.partial(fused_kernel, slabs, rows, head_dim ** (...  214 us
    unnamed x15, local copies, waits for them, and re-layouts  7.1 us

profile of v2, /device:TPU:1, one launch (start us, length us, event | category | flops | bytes accessed | tf_op | source)
XLA Modules:
  0.0 223.1 jit_solution(15064703621284916621)
XLA Ops:
  0.6 0.0 copy-start.4
  0.7 0.6 copy-done.4
  1.3 0.6 dynamic_slice.8
  1.9 0.0 copy-start.3
  1.9 0.7 copy-done.3
  2.6 0.1 reshape.69
  2.7 0.7 fusion.1
  3.4 0.1 broadcast_in_dim.12.shift_ref
  3.5 0.1 broadcast_in_dim.26.bias_ref
  3.5 0.0 copy-start
  3.5 1.2 copy.28
  4.7 0.0 copy-done
  4.7 0.0 copy-start.1
  4.7 0.0 copy-start.2
  4.7 0.2 copy.27
  5.0 0.8 copy-done.1
  5.8 0.2 copy-done.2
  5.9 0.1 copy_bitcast_fusion.1
  6.1 213.5 %shard_map.85 = (bf16[32,64,128]{2,1,0:T(8,128)(2,1)S(1)}, bf16[32,2,64,128]{3,2,1,0:T(8,128)(2,1)S(1)}) custom-call(f32[3,8,128]{2,1,0:T(8,128)S(1)} %broadcast_in_dim.12.shift_ref, f32[4,3,8,128]{3,2,1,0:T(8,128)S(1)} %broadcast_in_dim.26.bias_ref, bf16[2,1024,128]{2,1,0:T(8,128)(2,1)S(1)} %bitcast.20, bf16[2,1024,128]{2,1,0:T(8,128)(2,1)S(1)} %get-tuple-element.18.k_ref, ...), custom_call_target="tpu_custom_call" | custom-call | flops 4026531840 | bytes 8388608 | tf_op jit(solution)/shard_map/pallas_call | solution.py:332
  219.6 1.1 copy.20
  220.7 0.1 slice_bitcast_fusion
  220.8 1.1 copy.22
  221.9 1.1 copy.21
  (4 shorter events, 0.0 us)
Async XLA Ops:
  0.6 0.7 copy-start.4
  1.9 0.7 copy-start.3
  3.5 1.2 copy-start
  4.7 1.0 copy-start.1
  4.7 1.2 copy-start.2

commit v3 on v2

--- a/solution.py
+++ b/solution.py
@@ -12,6 +12,7 @@
 GW = 4
 WIN_COLS = 2
 TPS = 8
+RUN = 8
 NEG = -1e30
 LOG2E = 1.4426950408889634
 MESH = pl.DeviceIdType.MESH
@@ -36,6 +37,10 @@
     below = lax.rem(slab + slabs - 1, slabs)
     above = lax.rem(slab + 1, slabs)
     sides = (below, above)
+    half = rows // 2
+    group = row // half
+    mine, others = group * half, (1 - group) * half
+    edges = (slab % RUN == 0, slab % RUN == RUN - 1)
 
     def peer(step):
         return lax.rem(row + step, rows)
@@ -49,7 +54,21 @@
         return carry
 
     lax.fori_loop(1, rows, greet, 0)
-    pl.semaphore_wait(barrier, rows + 1)
+    for n in range(2):
+
+        @pl.when(edges[n])
+        def _():
+            def greet_far(step, carry):
+                pl.semaphore_signal(
+                    barrier, inc=1, device_id=(sides[n], others + step), device_id_type=MESH
+                )
+                return carry
+
+            lax.fori_loop(0, half, greet_far, 0)
+
+    at_edge = jnp.logical_or(edges[0], edges[1])
+    pl.semaphore_wait(barrier, rows + 1 + jnp.where(at_edge, half, 0))
+
 
     def to_side(src, dst, n, send, recv, head):
         return pltpu.make_async_remote_copy(
@@ -92,9 +111,45 @@
         pltpu.make_async_copy(whole, whole, recv.at[head]).wait()
         pltpu.make_async_copy(whole, whole, send.at[head]).wait()
 
+    def blocks_to_side(own, far, inbox, n, send, recv, head):
+        @pl.when(jnp.logical_not(edges[n]))
+        def _():
+            to_side(own, inbox.at[1 - n, head], n, send, recv, head).start()
+
+        @pl.when(edges[n])
+        def _():
+            near = pl.ds(mine, half)
+            to_side(own.at[near], inbox.at[1 - n, head, near], n, send, recv, head).start()
+            if far is not None:
+                far(n, head)
+
+    def far_copies(block_of, inbox, n, send, recv, head):
+        def one(step, carry):
+            other = others + step
+            pltpu.make_async_remote_copy(
+                src_ref=block_of(other),
+                dst_ref=inbox.at[1 - n, head, row],
+                send_sem=send.at[head, n],
+                recv_sem=recv.at[head, 1 - n],
+                device_id=(sides[n], other),
+                device_id_type=MESH,
+            ).start()
+            return carry
+
+        lax.fori_loop(0, half, one, 0)
+
+    def spread_far(head):
+        for n in range(2):
+
+            @pl.when(edges[n])
+            def _():
+                far_copies(
+                    lambda other: g_ref.at[other * heads + head], g_side, n, g_send, g_recv, head
+                )
+
     def send_grads(head):
         for n in range(2):
-            to_side(g_own.at[head], g_side.at[1 - n, head], n, g_send, g_recv, head).start()
+            blocks_to_side(g_own.at[head], None, g_side, n, g_send, g_recv, head)
 
     def pick(ref, head, tile, part):
         base = (tile % GW) // 2
@@ -143,8 +198,8 @@
             grad_attend = lax.dot_general(
                 values, grad_of(head, tile, part), NT, preferred_element_type=jnp.float32
             )
-            expo_ref[part, tile] = expo
-            gatt_ref[part, tile] = grad_attend
+            expo_ref[head, part, tile] = expo
+            gatt_ref[head, part, tile] = grad_attend
             at = pl.ds(tile, 1)
             stat[head, part, 0, at, :] = peak
             stat[head, part, 1, at, :] = jnp.sum(expo, axis=0, keepdims=True)
@@ -184,15 +239,18 @@
             keys = pick(k_ref, head, tile, part)
             src = final.at[head] if part == 1 else final_in.at[part // 2, head]
             scale = jnp.exp2(stat[head, part, 0, at, :] - src[0, at, :]) * src[1, at, :]
-            attend = expo_ref[part, tile] * scale
-            grad_scores = (attend * (gatt_ref[part, tile] - src[2, at, :])).astype(jnp.bfloat16)
+            attend = expo_ref[head, part, tile] * scale
+            grad_scores = (attend * (gatt_ref[head, part, tile] - src[2, at, :])).astype(jnp.bfloat16)
             attend_b = attend.astype(jnp.bfloat16)
             dq = lax.dot_general(grad_scores, keys, TN, preferred_element_type=jnp.float32)
             rows_at = pl.ds(pl.multiple_of(tile * TILE, TILE), TILE)
             if part == 1:
-                dq_own[rows_at, :] = dq * inv_root
+                dq_own[head, rows_at, :] = dq * inv_root
             else:
-                dq_side[part // 2, head, rows_at, :] = (dq * inv_root).astype(jnp.bfloat16)
+                each = TILE // block
+                dq_side[part // 2, head, pl.ds(tile * each, each)] = (
+                    (dq * inv_root).astype(jnp.bfloat16).reshape(each, block, head_dim)
+                )
             dk = jnp.dot(
                 grad_scores, query_of(head, tile, part), preferred_element_type=jnp.float32
             )
@@ -241,11 +299,13 @@
         lax.fori_loop(1, rows, one, 0)
         okv_ref[row * heads + head] = kv_out[head, row]
 
-    def send_dq(head):
-        for n in range(2):
-            to_side(
-                dq_side.at[n, head], dq_in.at[1 - n, head], n, dq_send, dq_recv, head
-            ).start()
+    def send_dq(head, n):
+        def far(n, head):
+            far_copies(
+                lambda other: dq_side.at[n, head, other], dq_in, n, dq_send, dq_recv, head
+            )
+
+        blocks_to_side(dq_side.at[n, head], far, dq_in, n, dq_send, dq_recv, head)
 
     def finish_dq(head):
         for n in range(2):
@@ -253,11 +313,10 @@
 
         def stage(other, carry):
             at = pl.ds(pl.multiple_of(other * block, block), block)
-            total = (
-                dq_mid[head][at, :]
-                + dq_in[0, head, at, :].astype(jnp.float32)
-                + dq_in[1, head, at, :].astype(jnp.float32)
-            )
+            total = dq_own[head, at, :]
+            for n in range(2):
+                here = jnp.logical_or(jnp.logical_not(edges[n]), other // half == group)
+                total += jnp.where(here, dq_in[n, head, other].astype(jnp.float32), 0.0)
             dq_out[head, other] = total.astype(jnp.bfloat16)
             return carry
 
@@ -278,34 +337,39 @@
         lax.fori_loop(1, rows, one, 0)
         oq_ref[row * heads + head] = dq_out[head, row]
 
-    dq_all = dq_own
-    dq_mid = [dq_all.at[head] for head in range(heads)]
-
-    send_queries(0)
-    spread_grad(0)
-    for head in range(heads):
-        await_spread(g_own.at[head], a_send, a_recv, head)
-        send_grads(head)
-        if head + 1 < heads:
-            spread_grad(head + 1)
-            send_queries(head + 1)
-
-    for head in range(heads):
-        dq_own = dq_mid[head]
-        acc[...] = jnp.zeros_like(acc)
-        first_pass(head, 1)
+    def sides_pass(head):
         for n in range(2):
             from_side(q_side.at[n, head], n, q_recv, head)
             from_side(g_side.at[n, head], n, g_recv, head)
             first_pass(head, 2 * n)
         send_stats(head)
-        combine(head)
-        second_pass(head, 1)
+
+    def results(head):
+        acc[...] = jnp.zeros_like(acc)
         for n in range(2):
             from_side(final_in.at[n, head], n, f_recv, head)
             second_pass(head, 2 * n)
-        send_dq(head)
+            send_dq(head, n)
+        second_pass(head, 1)
         send_home(head)
+
+    for head in range(heads):
+        spread_far(head)
+        spread_grad(head)
+    for head in range(heads):
+        send_queries(head)
+    await_spread(g_own.at[0], a_send, a_recv, 0)
+    send_grads(0)
+    first_pass(0, 1)
+    await_spread(g_own.at[1], a_send, a_recv, 1)
+    send_grads(1)
+    sides_pass(0)
+    first_pass(1, 1)
+    combine(0)
+    sides_pass(1)
+    results(0)
+    combine(1)
+    results(1)
     for head in range(heads):
         finish_dq(head)
 
@@ -319,6 +383,18 @@
         await_spread(kv_out.at[head], kv_send, kv_recv, head)
     for head in range(heads):
         await_spread(dq_out.at[head], o_send, o_recv, head)
+        for n in range(2):
+
+            @pl.when(edges[n])
+            def _():
+                def add(step, carry):
+                    other = others + step
+                    at = other * heads + head
+                    total = oq_ref[at].astype(jnp.float32) + dq_in[n, head, other].astype(jnp.float32)
+                    oq_ref[at] = total.astype(jnp.bfloat16)
+                    return carry
+
+                lax.fori_loop(0, half, add, 0)
 
 
 def fused_call(shift, bias, query, key, value, grad, slabs, rows):
@@ -329,6 +405,7 @@
     pairs = heads * tok_slab * 3 * keys_seen
     low, full = jnp.bfloat16, jnp.float32
     side = pltpu.VMEM((2, heads, tok_slab, head_dim), low)
+    blocks = pltpu.VMEM((2, heads, rows, block, head_dim), low)
     return pl.pallas_call(
         functools.partial(fused_kernel, slabs, rows, head_dim ** (-0.5)),
         out_shape=(
@@ -340,9 +417,9 @@
         scratch_shapes=[
             side,
             pltpu.VMEM((heads, rows, block, head_dim), low),
-            pltpu.VMEM((2, heads, rows, block, head_dim), low),
-            pltpu.VMEM((3, TPS, keys_seen, TILE), full),
-            pltpu.VMEM((3, TPS, keys_seen, TILE), full),
+            blocks,
+            pltpu.VMEM((heads, 3, TPS, keys_seen, TILE), full),
+            pltpu.VMEM((heads, 3, TPS, keys_seen, TILE), full),
             pltpu.VMEM((heads, 3, 3, TPS, TILE), full),
             pltpu.VMEM((2, heads, 3, TPS, TILE), full),
             pltpu.VMEM((heads, 3, TPS, TILE), full),
@@ -350,8 +427,8 @@
             pltpu.VMEM((2, tok_slab, head_dim), full),
             pltpu.VMEM((heads, rows, 2, block, head_dim), low),
             pltpu.VMEM((heads, tok_slab, head_dim), full),
-            side,
-            side,
+            blocks,
+            blocks,
             pltpu.VMEM((heads, rows, block, head_dim), low),
         ]
         + [

time: 223 us -> 201 us (0.901); the launches traced: 223 us -> 198 us
  Pallas kernels: 214 us -> 189 us
    pallas_call x1, Pallas kernels: 214 us -> 189 us  [fused_call(): pl.pallas_call(functools.partial(fused_kernel, slabs, rows, head_dim ** (...]
where the time goes in v3:
time: 201 us; the launch traced here: 198 us
  Pallas kernels  189 us (94%)
  local copies, waits for them, and re-layouts  8.12 us (4%)
    pallas_call x1, Pallas kernels, fused_call(): pl.pallas_call(functools.partial(fused_kernel, slabs, rows, head_dim ** (...  189 us
    unnamed x15, local copies, waits for them, and re-layouts  7.1 us

profile of v3, /device:TPU:1, one launch (start us, length us, event | category | flops | bytes accessed | tf_op | source)
XLA Modules:
  0.0 198.1 jit_solution(14678717084505911442)
XLA Ops:
  0.6 0.0 copy-start.4
  0.7 0.6 copy-done.4
  1.3 0.6 dynamic_slice.8
  1.9 0.0 copy-start.3
  1.9 0.7 copy-done.3
  2.6 0.1 reshape.69
  2.7 0.7 fusion.1
  3.4 0.1 broadcast_in_dim.12.shift_ref
  3.5 0.1 broadcast_in_dim.26.bias_ref
  3.5 0.0 copy-start
  3.5 1.2 copy.28
  4.7 0.0 copy-done
  4.7 0.0 copy-start.1
  4.7 0.0 copy-start.2
  4.7 0.2 copy.27
  5.0 0.8 copy-done.1
  5.8 0.2 copy-done.2
  5.9 0.1 copy_bitcast_fusion.1
  6.1 188.6 %shard_map.85 = (bf16[32,64,128]{2,1,0:T(8,128)(2,1)S(1)}, bf16[32,2,64,128]{3,2,1,0:T(8,128)(2,1)S(1)}) custom-call(f32[3,8,128]{2,1,0:T(8,128)S(1)} %broadcast_in_dim.12.shift_ref, f32[4,3,8,128]{3,2,1,0:T(8,128)S(1)} %broadcast_in_dim.26.bias_ref, bf16[2,1024,128]{2,1,0:T(8,128)(2,1)S(1)} %bitcast.20, bf16[2,1024,128]{2,1,0:T(8,128)(2,1)S(1)} %get-tuple-element.18.k_ref, ...), custom_call_target="tpu_custom_call" | custom-call | flops 4026531840 | bytes 8388608 | tf_op jit(solution)/shard_map/pallas_call | solution.py:409
  194.7 1.1 copy.20
  195.8 0.1 slice_bitcast_fusion
  195.9 1.1 copy.22
  197.0 1.1 copy.21
  (4 shorter events, 0.0 us)
Async XLA Ops:
  0.6 0.7 copy-start.4
  1.9 0.7 copy-start.3
  3.5 1.2 copy-start
  4.7 1.0 copy-start.1
  4.7 1.2 copy-start.2

commit v4 on v3

--- a/solution.py
+++ b/solution.py
@@ -21,11 +21,11 @@
 
 
 def fused_kernel(
-    slabs, rows, inv_root, shift_ref, bias_ref, q_ref, k_ref, v_ref, g_ref,
+    slabs, rows, inv_root, cols_ref, counts_ref, q_ref, k_ref, v_ref, g_ref,
     oq_ref, okv_ref,
-    q_side, g_own, g_side, expo_ref, gatt_ref, stat, stat_in, final, final_in,
+    q_side, g_own, g_side, expo_ref, gatt_ref, peaks, stat, stat_in, final,
     acc, kv_out, dq_own, dq_side, dq_in, dq_out,
-    q_send, q_recv, a_send, a_recv, g_send, g_recv, s_send, s_recv, f_send, f_recv,
+    q_send, q_recv, a_send, a_recv, g_send, g_recv, s_send, s_recv,
     kv_send, kv_recv, dq_send, dq_recv, o_send, o_recv,
 ):
     heads, tok_slab, head_dim = q_ref.shape
@@ -46,7 +46,9 @@
         return lax.rem(row + step, rows)
 
     barrier = pltpu.get_barrier_semaphore()
-    for side in sides:
+    two_below = lax.rem(slab + slabs - 2, slabs)
+    two_above = lax.rem(slab + 2, slabs)
+    for side in (two_below, below, above, two_above):
         pl.semaphore_signal(barrier, inc=1, device_id=(side, row), device_id_type=MESH)
 
     def greet(step, carry):
@@ -67,7 +69,7 @@
             lax.fori_loop(0, half, greet_far, 0)
 
     at_edge = jnp.logical_or(edges[0], edges[1])
-    pl.semaphore_wait(barrier, rows + 1 + jnp.where(at_edge, half, 0))
+    pl.semaphore_wait(barrier, rows + 3 + jnp.where(at_edge, half, 0))
 
 
     def to_side(src, dst, n, send, recv, head):
@@ -151,10 +153,24 @@
         for n in range(2):
             blocks_to_side(g_own.at[head], None, g_side, n, g_send, g_recv, head)
 
+    def first_of(tile, part):
+        owner = (below, slab, above)[part]
+        return jnp.full((1, TILE), cols_ref[owner * TPS + tile], jnp.int32)
+
+    def shift_of(tile, part):
+        return (first_of(tile, part) - (tile % GW) // 2).astype(jnp.float32)
+
+    limit = jnp.full((1, TILE), counts_ref[slab], jnp.int32)
+    inside = (slab > 0, None, slab < slabs - 1)
+
+    def bias_of(slot, tile, part):
+        reach = limit if part == 1 else jnp.where(inside[part], limit, 0)
+        inner = first_of(tile, part) + (slot // WIN_COLS * GW + slot % WIN_COLS)
+        return jnp.where(inner < reach, 0.0, NEG)
+
     def pick(ref, head, tile, part):
         base = (tile % GW) // 2
-        high = jnp.broadcast_to(shift_ref[part, pl.ds(tile, 1), :], (TILE, head_dim))
-        high = high.astype(jnp.bfloat16)
+        high = jnp.broadcast_to(shift_of(tile, part), (TILE, head_dim)).astype(jnp.bfloat16)
         low = 1 - high
         chosen = []
         for r in range(GH):
@@ -184,7 +200,7 @@
             values = pick(v_ref, head, tile, part)
             bias = jnp.concatenate(
                 [
-                    jnp.broadcast_to(bias_ref[n, part, pl.ds(tile, 1), :], (TILE, TILE))
+                    jnp.broadcast_to(bias_of(n, tile, part), (TILE, TILE))
                     for n in range(GH * WIN_COLS)
                 ],
                 axis=0,
@@ -201,46 +217,58 @@
             expo_ref[head, part, tile] = expo
             gatt_ref[head, part, tile] = grad_attend
             at = pl.ds(tile, 1)
-            stat[head, part, 0, at, :] = peak
-            stat[head, part, 1, at, :] = jnp.sum(expo, axis=0, keepdims=True)
-            stat[head, part, 2, at, :] = jnp.sum(expo * grad_attend, axis=0, keepdims=True)
+            total = jnp.sum(expo, axis=0, keepdims=True)
+            dot = jnp.sum(expo * grad_attend, axis=0, keepdims=True)
+            peaks[head, part, at, :] = peak
+            stat[head, part, 0, at, :] = peak + jnp.log2(total)
+            stat[head, part, 1, at, :] = dot / total
             return carry
 
         lax.fori_loop(0, TPS, one, 0)
 
+    routes = (
+        (1, above, 0, 0), (2, two_above, 0, 1), (0, below, 1, 0),
+        (2, above, 1, 1), (0, two_below, 2, 0), (1, below, 2, 1),
+    )
+
+    def stat_copy(head, route):
+        part, target, there, slot = route
+        return pltpu.make_async_remote_copy(
+            src_ref=stat.at[head, part],
+            dst_ref=stat_in.at[head, there, slot],
+            send_sem=s_send.at[head, there, slot],
+            recv_sem=s_recv.at[head, there, slot],
+            device_id=(target, row),
+            device_id_type=MESH,
+        )
+
     def send_stats(head):
-        for n in range(2):
-            to_side(
-                stat.at[head, 2 * n], stat_in.at[1 - n, head], n, s_send, s_recv, head
-            ).start()
-
-    def combine(head):
-        for n in range(2):
-            from_side(stat_in.at[n, head], n, s_recv, head)
-        peaks = [stat_in[0, head, 0], stat[head, 1, 0], stat_in[1, head, 0]]
-        sums = [stat_in[0, head, 1], stat[head, 1, 1], stat_in[1, head, 1]]
-        dots = [stat_in[0, head, 2], stat[head, 1, 2], stat_in[1, head, 2]]
-        top = jnp.maximum(jnp.maximum(peaks[0], peaks[1]), peaks[2])
-        weights = [jnp.exp2(p - top) for p in peaks]
-        total = sum(w * s for w, s in zip(weights, sums))
-        final[head, 0] = top
-        final[head, 1] = 1.0 / total
-        final[head, 2] = sum(w * d for w, d in zip(weights, dots)) / total
-        for n in range(2):
-            to_side(
-                final.at[head], final_in.at[1 - n, head], n, f_send, f_recv, head
-            ).start()
+        for route in routes:
+            stat_copy(head, route).start()
+
+    def combine(head, part):
+        for slot in range(2):
+            ref = stat_in.at[head, part, slot]
+            pltpu.make_async_copy(ref, ref, s_recv.at[head, part, slot]).wait()
+        logs = [stat[head, part, 0], stat_in[head, part, 0, 0], stat_in[head, part, 1, 0]]
+        dots = [stat[head, part, 1], stat_in[head, part, 0, 1], stat_in[head, part, 1, 1]]
+        top = jnp.maximum(jnp.maximum(logs[0], logs[1]), logs[2])
+        weights = [jnp.exp2(one - top) for one in logs]
+        total = weights[0] + weights[1] + weights[2]
+        final[head, part, 0] = jnp.exp2(peaks[head, part] - top) / total
+        final[head, part, 1] = (
+            weights[0] * dots[0] + weights[1] * dots[1] + weights[2] * dots[2]
+        ) / total
 
     def second_pass(head, part):
         def one(tile, carry):
             base = (tile % GW) // 2
             at = pl.ds(tile, 1)
-            shifted = jnp.broadcast_to(shift_ref[part, at, :], (TILE, head_dim)) > 0.5
+            shifted = jnp.broadcast_to(shift_of(tile, part), (TILE, head_dim)) > 0.5
             keys = pick(k_ref, head, tile, part)
-            src = final.at[head] if part == 1 else final_in.at[part // 2, head]
-            scale = jnp.exp2(stat[head, part, 0, at, :] - src[0, at, :]) * src[1, at, :]
-            attend = expo_ref[head, part, tile] * scale
-            grad_scores = (attend * (gatt_ref[head, part, tile] - src[2, at, :])).astype(jnp.bfloat16)
+            attend = expo_ref[head, part, tile] * final[head, part, 0, at, :]
+            grad_scores = attend * (gatt_ref[head, part, tile] - final[head, part, 1, at, :])
+            grad_scores = grad_scores.astype(jnp.bfloat16)
             attend_b = attend.astype(jnp.bfloat16)
             dq = lax.dot_general(grad_scores, keys, TN, preferred_element_type=jnp.float32)
             rows_at = pl.ds(pl.multiple_of(tile * TILE, TILE), TILE)
@@ -347,9 +375,10 @@
     def results(head):
         acc[...] = jnp.zeros_like(acc)
         for n in range(2):
-            from_side(final_in.at[n, head], n, f_recv, head)
+            combine(head, 2 * n)
             second_pass(head, 2 * n)
             send_dq(head, n)
+        combine(head, 1)
         second_pass(head, 1)
         send_home(head)
 
@@ -365,10 +394,8 @@
     send_grads(1)
     sides_pass(0)
     first_pass(1, 1)
-    combine(0)
     sides_pass(1)
     results(0)
-    combine(1)
     results(1)
     for head in range(heads):
         finish_dq(head)
@@ -377,9 +404,9 @@
         for n in range(2):
             to_side(q_ref.at[head], q_side.at[1 - n, head], n, q_send, q_recv, head).wait_send()
             to_side(g_own.at[head], g_side.at[1 - n, head], n, g_send, g_recv, head).wait_send()
-            to_side(stat.at[head, 2 * n], stat_in.at[1 - n, head], n, s_send, s_recv, head).wait_send()
-            to_side(final.at[head], final_in.at[1 - n, head], n, f_send, f_recv, head).wait_send()
             to_side(dq_side.at[n, head], dq_in.at[1 - n, head], n, dq_send, dq_recv, head).wait_send()
+        for route in routes:
+            stat_copy(head, route).wait_send()
         await_spread(kv_out.at[head], kv_send, kv_recv, head)
     for head in range(heads):
         await_spread(dq_out.at[head], o_send, o_recv, head)
@@ -397,10 +424,11 @@
                 lax.fori_loop(0, half, add, 0)
 
 
-def fused_call(shift, bias, query, key, value, grad, slabs, rows):
+def fused_call(cols, counts, query, key, value, grad, slabs, rows):
     heads, tok_slab, head_dim = query.shape
     block = grad.shape[1]
     vmem = pl.BlockSpec(memory_space=pltpu.VMEM)
+    smem = pl.BlockSpec(memory_space=pltpu.SMEM)
     keys_seen = GH * WIN_COLS * TILE
     pairs = heads * tok_slab * 3 * keys_seen
     low, full = jnp.bfloat16, jnp.float32
@@ -412,7 +440,7 @@
             jax.ShapeDtypeStruct((rows * heads, block, head_dim), low),
             jax.ShapeDtypeStruct((rows * heads, 2, block, head_dim), low),
         ),
-        in_specs=[vmem] * 6,
+        in_specs=[smem] * 2 + [vmem] * 4,
         out_specs=(vmem, vmem),
         scratch_shapes=[
             side,
@@ -420,10 +448,10 @@
             blocks,
             pltpu.VMEM((heads, 3, TPS, keys_seen, TILE), full),
             pltpu.VMEM((heads, 3, TPS, keys_seen, TILE), full),
-            pltpu.VMEM((heads, 3, 3, TPS, TILE), full),
-            pltpu.VMEM((2, heads, 3, TPS, TILE), full),
             pltpu.VMEM((heads, 3, TPS, TILE), full),
-            pltpu.VMEM((2, heads, 3, TPS, TILE), full),
+            pltpu.VMEM((heads, 3, 2, TPS, TILE), full),
+            pltpu.VMEM((heads, 3, 2, 2, TPS, TILE), full),
+            pltpu.VMEM((heads, 3, 2, TPS, TILE), full),
             pltpu.VMEM((2, tok_slab, head_dim), full),
             pltpu.VMEM((heads, rows, 2, block, head_dim), low),
             pltpu.VMEM((heads, tok_slab, head_dim), full),
@@ -435,8 +463,7 @@
             pltpu.SemaphoreType.DMA((heads, 2)), pltpu.SemaphoreType.DMA((heads, 2)),
             pltpu.SemaphoreType.DMA((heads,)), pltpu.SemaphoreType.DMA((heads,)),
             pltpu.SemaphoreType.DMA((heads, 2)), pltpu.SemaphoreType.DMA((heads, 2)),
-            pltpu.SemaphoreType.DMA((heads, 2)), pltpu.SemaphoreType.DMA((heads, 2)),
-            pltpu.SemaphoreType.DMA((heads, 2)), pltpu.SemaphoreType.DMA((heads, 2)),
+            pltpu.SemaphoreType.DMA((heads, 3, 2)), pltpu.SemaphoreType.DMA((heads, 3, 2)),
             pltpu.SemaphoreType.DMA((heads,)), pltpu.SemaphoreType.DMA((heads,)),
             pltpu.SemaphoreType.DMA((heads, 2)), pltpu.SemaphoreType.DMA((heads, 2)),
             pltpu.SemaphoreType.DMA((heads,)), pltpu.SemaphoreType.DMA((heads,)),
@@ -447,29 +474,12 @@
         cost_estimate=pl.CostEstimate(
             flops=10 * pairs * head_dim, bytes_accessed=8 * 2**20, transcendentals=pairs
         ),
-    )(shift, bias, query, key, value, grad)
-
-
-def window_terms(slabs, col_start, valid_tiles):
-    slab = lax.axis_index("slab")
-    tile = jnp.arange(TPS, dtype=jnp.int32)
-    owners = slab + jnp.arange(-1, 2, dtype=jnp.int32)
-    inside = (owners >= 0) & (owners < slabs)
-    padded = jnp.pad(col_start.reshape(slabs, TPS), ((1, 1), (0, 0)))
-    first = lax.dynamic_slice_in_dim(padded, slab, 3, 0)
-    shift = first - (tile % GW) // 2
-    slot = jnp.arange(GH * WIN_COLS, dtype=jnp.int32)
-    inner = (slot // WIN_COLS * GW + slot % WIN_COLS)[:, None, None] + first
-    limit = lax.dynamic_index_in_dim(valid_tiles, slab, 0, False)
-    bias = jnp.where((inner < limit) & inside[:, None], 0.0, NEG)
-    wide = lambda a: jnp.broadcast_to(a.astype(jnp.float32)[..., None], a.shape + (TILE,))
-    return wide(shift), wide(bias)
+    )(cols, counts, query, key, value, grad)
 
 
 def on_device(slabs, rows, queries, keys, values, out_grad, col_start, valid_tiles):
-    shift, bias = window_terms(slabs, col_start, valid_tiles)
     dq, dkv = fused_call(
-        shift, bias, queries.swapaxes(0, 1), keys.swapaxes(0, 1),
+        col_start, valid_tiles, queries.swapaxes(0, 1), keys.swapaxes(0, 1),
         values.swapaxes(0, 1), out_grad.swapaxes(0, 1), slabs, rows,
     )
     return dq.swapaxes(0, 1), dkv[:, 0].swapaxes(0, 1), dkv[:, 1].swapaxes(0, 1)

time: 201 us -> 193 us (0.960); the launches traced: 198 us -> 193 us
  Pallas kernels: 189 us -> 185 us
    pallas_call x1, Pallas kernels: 189 us -> 185 us  [fused_call(): pl.pallas_call(functools.partial(fused_kernel, slabs, rows, head_dim ** (...]
where the time goes in v4:
time: 193 us
  Pallas kernels  185 us (96%)
  local copies, waits for them, and re-layouts  6.66 us (3%)
    pallas_call x1, Pallas kernels, fused_call(): pl.pallas_call(functools.partial(fused_kernel, slabs, rows, head_dim ** (...  185 us
    unnamed x15, local copies, waits for them, and re-layouts  6.45 us

profile of v4, /device:TPU:1, one launch (start us, length us, event | category | flops | bytes accessed | tf_op | source)
XLA Modules:
  0.0 192.7 jit_solution(8232953186459369751)
XLA Ops:
  0.6 0.0 copy-start.2
  0.6 1.2 copy.21
  1.8 0.0 copy-done.2
  1.8 0.0 copy-start.3
  1.8 0.0 copy-start.4
  1.8 0.2 copy.20
  2.1 0.8 copy-done.3
  2.9 0.2 copy-done.4
  3.0 0.1 copy_bitcast_fusion.1
  3.2 0.0 copy-start
  3.2 0.0 copy-start.1
  3.2 0.7 copy-done
  3.9 0.0 copy-done.1
  3.9 185.4 %shard_map.85 = (bf16[32,64,128]{2,1,0:T(8,128)(2,1)S(1)}, bf16[32,2,64,128]{3,2,1,0:T(8,128)(2,1)S(1)}) custom-call(s32[256]{0:T(256)S(1)} %copy-done, s32[32]{0:T(128)S(1)} %copy-done.1, bf16[2,1024,128]{2,1,0:T(8,128)(2,1)S(1)} %bitcast.19, bf16[2,1024,128]{2,1,0:T(8,128)(2,1)S(1)} %get-tuple-element.13.k_ref, ...), custom_call_target="tpu_custom_call" | custom-call | flops 4026531840 | bytes 8388608 | tf_op jit(solution)/shard_map/pallas_call | solution.py:437
  189.2 1.1 copy.13
  190.4 0.1 slice_bitcast_fusion
  190.4 1.1 copy.15
  191.6 1.1 copy.14
Async XLA Ops:
  0.6 1.2 copy-start.2
  1.8 1.0 copy-start.3
  1.8 1.2 copy-start.4
  3.2 0.7 copy-start
  3.2 0.7 copy-start.1

commit v5 on v4

--- a/solution.py
+++ b/solution.py
@@ -90,7 +90,21 @@
 
     def send_queries(head):
         for n in range(2):
-            to_side(q_ref.at[head], q_side.at[1 - n, head], n, q_send, q_recv, head).start()
+
+            @pl.when(jnp.logical_not(edges[n]))
+            def _():
+                to_side(q_ref.at[head], q_side.at[1 - n, head], n, q_send, q_recv, head).start()
+
+            @pl.when(edges[n])
+            def _():
+                def piece(step, carry):
+                    at = pl.ds(pl.multiple_of(step * block, block), block)
+                    to_side(
+                        q_ref.at[head, at], q_side.at[1 - n, head, at], n, q_send, q_recv, head
+                    ).start()
+                    return carry
+
+                lax.fori_loop(0, rows, piece, 0)
 
     def spread_grad(head):
         def one(step, carry):
@@ -120,8 +134,12 @@
 
         @pl.when(edges[n])
         def _():
-            near = pl.ds(mine, half)
-            to_side(own.at[near], inbox.at[1 - n, head, near], n, send, recv, head).start()
+            def piece(step, carry):
+                near = mine + step
+                to_side(own.at[near], inbox.at[1 - n, head, near], n, send, recv, head).start()
+                return carry
+
+            lax.fori_loop(0, half, piece, 0)
             if far is not None:
                 far(n, head)
 

time: 193 us -> 193 us (level)
  no operation moved by 1% of the time
where the time goes in v5:
time: 193 us
  Pallas kernels  185 us (96%)
  local copies, waits for them, and re-layouts  6.66 us (3%)
    pallas_call x1, Pallas kernels, fused_call(): pl.pallas_call(functools.partial(fused_kernel, slabs, rows, head_dim ** (...  185 us
    unnamed x15, local copies, waits for them, and re-layouts  6.45 us

profile of v5, /device:TPU:1, one launch (start us, length us, event | category | flops | bytes accessed | tf_op | source)
XLA Modules:
  0.0 192.8 jit_solution(17936762063756658941)
XLA Ops:
  0.6 0.0 copy-start.2
  0.6 1.2 copy.21
  1.8 0.0 copy-done.2
  1.8 0.0 copy-start.3
  1.8 0.0 copy-start.4
  1.8 0.2 copy.20
  2.1 0.8 copy-done.3
  2.9 0.2 copy-done.4
  3.0 0.1 copy_bitcast_fusion.1
  3.2 0.0 copy-start
  3.2 0.0 copy-start.1
  3.2 0.7 copy-done
  3.9 0.0 copy-done.1
  3.9 185.4 %shard_map.85 = (bf16[32,64,128]{2,1,0:T(8,128)(2,1)S(1)}, bf16[32,2,64,128]{3,2,1,0:T(8,128)(2,1)S(1)}) custom-call(s32[256]{0:T(256)S(1)} %copy-done, s32[32]{0:T(128)S(1)} %copy-done.1, bf16[2,1024,128]{2,1,0:T(8,128)(2,1)S(1)} %bitcast.19, bf16[2,1024,128]{2,1,0:T(8,128)(2,1)S(1)} %get-tuple-element.13.k_ref, ...), custom_call_target="tpu_custom_call" | custom-call | flops 4026531840 | bytes 8388608 | tf_op jit(solution)/shard_map/pallas_call | solution.py:455
  189.3 1.1 copy.13
  190.4 0.1 slice_bitcast_fusion
  190.5 1.1 copy.15
  191.6 1.1 copy.14
Async XLA Ops:
  0.6 1.2 copy-start.2
  1.8 1.0 copy-start.3
  1.8 1.2 copy-start.4
  3.2 0.7 copy-start
  3.2 0.7 copy-start.1

commit v6 on v4

--- a/solution.py
+++ b/solution.py
@@ -380,7 +380,6 @@
             send_dq(head, n)
         combine(head, 1)
         second_pass(head, 1)
-        send_home(head)
 
     for head in range(heads):
         spread_far(head)
@@ -396,9 +395,11 @@
     first_pass(1, 1)
     sides_pass(1)
     results(0)
+    send_home(0)
     results(1)
     for head in range(heads):
         finish_dq(head)
+    send_home(1)
 
     for head in range(heads):
         for n in range(2):

time: 193 us -> 193 us (level); the launches traced: 193 us -> 190 us
  Pallas kernels: 185 us -> 183 us
    pallas_call x1, Pallas kernels: 185 us -> 183 us  [fused_call(): pl.pallas_call(functools.partial(fused_kernel, slabs, rows, head_dim ** (...]
where the time goes in v6:
time: 193 us; the launch traced here: 190 us
  Pallas kernels  183 us (95%)
  local copies, waits for them, and re-layouts  6.66 us (3%)
    pallas_call x1, Pallas kernels, fused_call(): pl.pallas_call(functools.partial(fused_kernel, slabs, rows, head_dim ** (...  183 us
    unnamed x15, local copies, waits for them, and re-layouts  6.45 us

profile of v6, /device:TPU:1, one launch (start us, length us, event | category | flops | bytes accessed | tf_op | source)
XLA Modules:
  0.0 190.1 jit_solution(698738482874538507)
XLA Ops:
  0.6 0.0 copy-start.2
  0.6 1.2 copy.21
  1.8 0.0 copy-done.2
  1.8 0.0 copy-start.3
  1.8 0.0 copy-start.4
  1.8 0.2 copy.20
  2.1 0.8 copy-done.3
  2.9 0.2 copy-done.4
  3.0 0.1 copy_bitcast_fusion.1
  3.2 0.0 copy-start
  3.2 0.0 copy-start.1
  3.2 0.7 copy-done
  3.9 0.0 copy-done.1
  3.9 182.7 %shard_map.85 = (bf16[32,64,128]{2,1,0:T(8,128)(2,1)S(1)}, bf16[32,2,64,128]{3,2,1,0:T(8,128)(2,1)S(1)}) custom-call(s32[256]{0:T(256)S(1)} %copy-done, s32[32]{0:T(128)S(1)} %copy-done.1, bf16[2,1024,128]{2,1,0:T(8,128)(2,1)S(1)} %bitcast.19, bf16[2,1024,128]{2,1,0:T(8,128)(2,1)S(1)} %get-tuple-element.13.k_ref, ...), custom_call_target="tpu_custom_call" | custom-call | flops 4026531840 | bytes 8388608 | tf_op jit(solution)/shard_map/pallas_call | solution.py:438
  186.6 1.1 copy.13
  187.7 0.1 slice_bitcast_fusion
  187.8 1.1 copy.15
  188.9 1.1 copy.14
Async XLA Ops:
  0.6 1.2 copy-start.2
  1.8 1.0 copy-start.3
  1.8 1.2 copy-start.4
  3.2 0.7 copy-start
  3.2 0.7 copy-start.1
